TPU v7x, 32 devices: a whole 2x2x4 slice. The times are simulated.
32 devices in a mesh: dp: 2 (over x), blk: 16 (over z, y, core).
Axes of the slice: x: 2, y: 2, z: 4, core: 2. Of those that a mesh axis runs over, the one named last changes fastest.
Arguments:
- decoder_rows: bfloat16 [32768, 768], P(('dp', 'blk')), may hold values from -6 to 6
- encoder_rows: bfloat16 [2048, 768], P(('dp', 'blk')), may hold values from -6 to 6
- target_lengths: int32 [32, 4], P(('dp', 'blk')), may hold values from 1 to 512, 1024 in all within a row
- target_question: int32 [32, 4], P(('dp', 'blk')), may hold values from 0 to 3, each once within a row
- passage_question: int32 [32], P('dp'), may hold values from 0 to 3, as said below
- self_gain: float32 [768], replicated, may hold values from 0.1 to 1.9
- self_query: bfloat16 [768, 768], replicated, may hold values from -0.4375 to 0.4375
- self_key: bfloat16 [768, 768], replicated, may hold values from -0.21875 to 0.21875
- self_value: bfloat16 [768, 768], replicated, may hold values from -0.21875 to 0.21875
- self_output: bfloat16 [768, 768], replicated, may hold values from -0.875 to 0.875
- position_bias_matrix: bfloat16 [32, 12], replicated, may hold values from -4 to 4
- cross_gain: float32 [768], replicated, may hold values from 0.1 to 1.9
- cross_query: bfloat16 [768, 768], replicated, may hold values from -0.4375 to 0.4375
- cross_key: bfloat16 [768, 768], replicated, may hold values from -0.21875 to 0.21875
- cross_value: bfloat16 [768, 768], replicated, may hold values from -0.21875 to 0.21875
- cross_output: bfloat16 [768, 768], replicated, may hold values from -0.875 to 0.875
- feed_gain: float32 [768], replicated, may hold values from 0.1 to 1.9
- feed_input_weight: bfloat16 [768, 3072], replicated, may hold values from -0.21875 to 0.21875
- feed_out: bfloat16 [3072, 768], replicated, may hold values from -0.109375 to 0.109375
- cotangent: bfloat16 [32768, 768], P(('dp', 'blk')), may hold values from -6 to 6
Outputs:
- block_out: bfloat16 [32768, 768], P(('dp', 'blk'))
- grad_decoder: float32 [32768, 768], P(('dp', 'blk'))
- grad_encoder: float32 [2048, 768], P(('dp', 'blk'))
- grad_self_gain: float32 [768], replicated
- grad_self_query: float32 [768, 768], P('blk')
- grad_self_key: float32 [768, 768], P('blk')
- grad_self_value: float32 [768, 768], P('blk')
- grad_self_output: float32 [768, 768], P('blk')
- grad_bias_table: float32 [32, 12], replicated
- grad_cross_gain: float32 [768], replicated
- grad_cross_query: float32 [768, 768], P('blk')
- grad_cross_key: float32 [768, 768], P('blk')
- grad_cross_value: float32 [768, 768], P('blk')
- grad_cross_output: float32 [768, 768], P('blk')
- grad_feed_gain: float32 [768], replicated
- grad_feed_in: float32 [768, 3072], P('blk')
- grad_feed_out: float32 [3072, 768], P('blk')
Inputs may be any that keep to these rules, and one draw needn't show every extreme that they name: `target_lengths`: the 4 lengths of a sequence sum to 1024; in every sequence the largest is exactly 512. `target_question`: each row is a permutation of the 4 questions. `passage_question`: within the 16 passages of one dp index, each of the 4 questions owns exactly 4 passages.
All inputs are finite; a program needn't handle non-finite values.
Results may differ from a plain program's by a relative error of at most 0.029.
The roundings to bfloat16 on the way count: a program that leaves them out, or rounds other values in their place, can miss the bound.
Values may be sent and summed in bfloat16 or wider, within the bound.
A program may use at most 576 MiB of HBM per device.

v0:
```python
import functools
from functools import partial

import jax
import jax.numpy as jnp
from jax import lax
from jax.experimental import pallas as pl
from jax.experimental.pallas import tpu as pltpu
from jax.sharding import PartitionSpec as P

D = 768
H = 12
HD = 64
BUCKETS = 32
LEN = 1024
TARGETS = 4
PAIRS = H // 2
LANES = 2 * HD
TILE = 256
SCALE = HD ** -0.5
NEG = -1e30
VMEM_LIMIT = 60 * 1024 * 1024

eps_norm = 1e-06
bucket_edges = (19, 21, 24, 27, 31, 35, 40, 46, 52, 59, 67, 77, 87, 99, 113)


def dot_nn(a, b):
    return jnp.dot(a, b, preferred_element_type=jnp.float32)


def dot_nt(a, b):
    return lax.dot_general(a, b, (((1,), (1,)), ((), ())), preferred_element_type=jnp.float32)


def dot_tn(a, b):
    return lax.dot_general(a, b, (((0,), (0,)), ((), ())), preferred_element_type=jnp.float32)


def lane_ids(rows):
    return lax.broadcasted_iota(jnp.int32, (rows, LANES), 1)


def in_half(rows, head):
    lane = lane_ids(rows)
    return lane < HD if head == 0 else lane >= HD


def split3(value):
    high = value.astype(jnp.bfloat16).astype(jnp.float32)
    rest = value - high
    mid = rest.astype(jnp.bfloat16).astype(jnp.float32)
    return high, mid, rest - mid


def triple_lanes(first, second, rows):
    lane = lane_ids(rows)
    out = jnp.zeros((rows, LANES), jnp.float32)
    for base, value in ((HD, first), (0, second)):
        for place, part in enumerate(split3(value)):
            out = jnp.where(lane == base + place, part, out)
    return out


def bucket_vector(table_t, offsets):
    upper = jnp.full(offsets.shape, 16, jnp.int32)
    for edge in bucket_edges:
        upper = upper + (offsets >= edge).astype(jnp.int32)
    bucket = jnp.where(offsets < 16, offsets, upper)
    rows = lax.broadcasted_iota(jnp.int32, (BUCKETS, offsets.shape[1]), 0)
    chosen = (rows == bucket).astype(jnp.float32).astype(jnp.bfloat16)
    return chosen


WIN = 3 * TILE


def self_forward_kernel(q_ref, k_ref, v_ref, aq_ref, ak_ref, table_ref, o_ref, aug_ref, bias_ref):
    lane768 = lax.broadcasted_iota(jnp.int32, (1, WIN), 1)
    offsets = 2 * TILE - lane768
    chosen = bucket_vector(None, jnp.maximum(offsets, 0))
    line = dot_nn(table_ref[0], chosen)
    line = jnp.where(offsets >= 0, line, NEG)
    far = table_ref[0][:, BUCKETS - 1 :].astype(jnp.float32)
    for head in range(2):
        spread = jnp.broadcast_to(line[head : head + 1], (TILE, WIN))
        bias_ref[head] = pltpu.roll(spread, 0, 1, stride=1, stride_axis=0)[:, TILE:]
    aq, ak = aq_ref[...], ak_ref[...]
    outs = {}
    logs = {}
    for head in range(2):
        half = in_half(LEN, head)
        q = jnp.where(half, q_ref[...] * jnp.bfloat16(SCALE), aq)
        k = jnp.where(half, k_ref[...], ak)
        v = jnp.where(half, v_ref[...], jnp.zeros((), jnp.bfloat16))
        for i in range(LEN // TILE):
            lo = max(0, i - 2) * TILE
            hi = (i + 1) * TILE
            scores = dot_nt(q[i * TILE : hi], k[lo:hi])
            near = min(2 * TILE, hi - lo)
            parts = []
            if hi - lo > near:
                parts.append(scores[:, : hi - lo - near] + far[head : head + 1])
            parts.append(scores[:, hi - lo - near :] + bias_ref[head][:, 2 * TILE - near :])
            scores = parts[0] if len(parts) == 1 else jnp.concatenate(parts, axis=1)
            top = jnp.max(scores, axis=1, keepdims=True)
            expo = jnp.exp(scores - top)
            total = jnp.sum(expo, axis=1, keepdims=True)
            mixed = dot_nn(expo.astype(jnp.bfloat16), v[lo:hi]) / total
            logs[i, head] = top + jnp.log(total)
            outs[i, head] = mixed
            if head == 1:
                o_ref[i * TILE : hi] = (outs[i, 0] + outs[i, 1]).astype(jnp.bfloat16)
                aug = triple_lanes(logs[i, 0], logs[i, 1], TILE)
                lane = lane_ids(TILE)
                place = lane & (HD - 1)
                aug_ref[i * TILE : hi] = jnp.where(
                    place < 3, aug, aq_ref[i * TILE : hi].astype(jnp.float32)
                ).astype(jnp.bfloat16)


def pair_spec(offset=0):
    return pl.BlockSpec((LEN, LANES), lambda p: (0, p + offset))


def whole(shape):
    return pl.BlockSpec(shape, lambda p: (0,) * len(shape))


def self_forward(q, k, v, aq, ak, table_pairs):
    return pl.pallas_call(
        self_forward_kernel,
        grid=(PAIRS,),
        in_specs=[pair_spec()] * 3 + [whole((LEN, LANES))] * 2
        + [pl.BlockSpec((1, 2, BUCKETS), lambda p: (p, 0, 0))],
        out_specs=[pair_spec(), pair_spec()],
        out_shape=[jax.ShapeDtypeStruct((LEN, D), jnp.bfloat16)] * 2,
        scratch_shapes=[pltpu.VMEM((2, TILE, 2 * TILE), jnp.float32)],
        compiler_params=pltpu.CompilerParams(vmem_limit_bytes=VMEM_LIMIT),
        cost_estimate=pl.CostEstimate(flops=4 * H * LEN * LEN * HD, bytes_accessed=10 * LEN * D, transcendentals=0),
    )(q, k, v, aq, ak, table_pairs)


def self_backward_kernel(q_ref, k_ref, v_ref, do_ref, o_ref, aug_ref, ak_ref, av_ref, table_ref,
                         dq_ref, dk_ref, dv_ref, gt_ref, bias_ref, g_ref, gfar_ref, dqt_ref):
    lane768 = lax.broadcasted_iota(jnp.int32, (1, WIN), 1)
    offsets = lane768 - TILE
    chosen = bucket_vector(None, jnp.maximum(offsets, 0))
    line = dot_nn(table_ref[0], chosen)
    line = jnp.where(offsets >= 0, line, NEG)
    far = table_ref[0][:, BUCKETS - 1 :].astype(jnp.float32)
    for head in range(2):
        spread = jnp.broadcast_to(line[head : head + 1], (TILE, WIN))
        bias_ref[head] = pltpu.roll(spread, 0, 1, stride=1, stride_axis=0)[:, TILE:]
    g_ref[...] = jnp.zeros_like(g_ref)
    gfar_ref[...] = jnp.zeros_like(gfar_ref)
    dqt_ref[...] = jnp.zeros_like(dqt_ref)
    product = do_ref[...].astype(jnp.float32) * o_ref[...].astype(jnp.float32)
    deltas = []
    for head in range(2):
        half = in_half(LEN, head)
        deltas.append(jnp.sum(jnp.where(half, product, 0.0), axis=1, keepdims=True))
    aug_do = (-triple_lanes(deltas[0], deltas[1], LEN)).astype(jnp.bfloat16)
    q_scaled = q_ref[...] * jnp.bfloat16(SCALE)
    k_t = k_ref[...].T
    accs = {}
    for head in range(2):
        half = in_half(LEN, head)
        q = jnp.where(half, q_scaled, aug_ref[...])
        k = jnp.where(half, k_ref[...], ak_ref[...])
        v = jnp.where(half, v_ref[...], av_ref[...])
        do = jnp.where(half, do_ref[...], aug_do)
        for j in range(LEN // TILE):
            lo = j * TILE
            hi = min(LEN, (j + 3) * TILE)
            width = hi - lo
            near = min(2 * TILE, width)
            scores = dot_nt(k[lo : lo + TILE], q[lo:hi])
            parts = [scores[:, :near] + bias_ref[head][:, :near]]
            if width > near:
                parts.append(scores[:, near:] + far[head : head + 1])
            scores = parts[0] if len(parts) == 1 else jnp.concatenate(parts, axis=1)
            probs = jnp.exp(scores)
            grad_probs = dot_nt(v[lo : lo + TILE], do[lo:hi])
            grad_scores = probs * grad_probs
            g_ref[head, :, :near] += grad_scores[:, :near]
            if width > near:
                gfar_ref[head] += grad_scores[:, near:]
            ds = grad_scores.astype(jnp.bfloat16)
            accs[j, head] = (dot_nn(ds, q[lo:hi]), dot_nn(probs.astype(jnp.bfloat16), do[lo:hi]))
            dqt_ref[head * HD : (head + 1) * HD, lo:hi] += dot_nn(
                k_t[head * HD : (head + 1) * HD, lo : lo + TILE], ds
            )
            if head == 1:
                lower = in_half(TILE, 0)
                dk_ref[lo : lo + TILE] = jnp.where(lower, accs[j, 0][0], accs[j, 1][0]).astype(jnp.bfloat16)
                dv_ref[lo : lo + TILE] = jnp.where(lower, accs[j, 0][1], accs[j, 1][1]).astype(jnp.bfloat16)
    dq_ref[...] = (dqt_ref[...] * SCALE).T.astype(jnp.bfloat16)
    rows = []
    for head in range(2):
        total = jnp.zeros((8, WIN), jnp.float32)
        pad = jnp.zeros((8, TILE), jnp.float32)
        for a in range(TILE // 8):
            strip = jnp.concatenate([pad, g_ref[head, 8 * a : 8 * a + 8, :]], axis=1)
            if a:
                strip = pltpu.roll(strip, WIN - 8 * a, 1)
            total = total + strip
        line_sum = jnp.zeros((1, WIN), jnp.float32)
        for s in range(8):
            one = total[s : s + 1]
            line_sum = line_sum + (pltpu.roll(one, WIN - s, 1) if s else one)
        rows.append(line_sum)
    lines = jnp.concatenate(rows, axis=0)
    lines = jnp.where(offsets >= 0, lines, 0.0)
    high, mid, low = split3(lines)
    sums = sum(dot_nt(part.astype(jnp.bfloat16), chosen) for part in (high, mid, low))
    for head in range(2):
        far_sum = jnp.sum(gfar_ref[head])
        lane32 = lax.broadcasted_iota(jnp.int32, (1, BUCKETS), 1)
        gt_ref[0, head : head + 1, :] = sums[head : head + 1] + jnp.where(lane32 == BUCKETS - 1, far_sum, 0.0)


def self_backward(q, k, v, do, o, aug, ak, av, table_pairs):
    return pl.pallas_call(
        self_backward_kernel,
        grid=(PAIRS,),
        in_specs=[pair_spec()] * 6 + [whole((LEN, LANES))] * 2
        + [pl.BlockSpec((1, 2, BUCKETS), lambda p: (p, 0, 0))],
        out_specs=[pair_spec()] * 3 + [pl.BlockSpec((1, 2, BUCKETS), lambda p: (p, 0, 0))],
        out_shape=[jax.ShapeDtypeStruct((LEN, D), jnp.bfloat16)] * 3
        + [jax.ShapeDtypeStruct((PAIRS, 2, BUCKETS), jnp.float32)],
        scratch_shapes=[
            pltpu.VMEM((2, TILE, 2 * TILE), jnp.float32),
            pltpu.VMEM((2, TILE, 2 * TILE), jnp.float32),
            pltpu.VMEM((2, TILE, TILE), jnp.float32),
            pltpu.VMEM((LANES, LEN), jnp.float32),
        ],
        compiler_params=pltpu.CompilerParams(vmem_limit_bytes=VMEM_LIMIT),
        cost_estimate=pl.CostEstimate(flops=10 * H * LEN * LEN * HD, bytes_accessed=18 * LEN * D, transcendentals=0),
    )(q, k, v, do, o, aug, ak, av, table_pairs)


CT = 256


def cross_forward_kernel(order_ref, item_ref, q_ref, kv_ref, o_ref, aug_ref, ks_ref, vs_ref, passage):
    slots = order_ref.shape[0]
    per_q = slots // TARGETS
    keys_q = per_q * passage
    lower = lax.broadcasted_iota(jnp.int32, (passage, D), 1) % LANES < HD
    zero = jnp.zeros((), jnp.bfloat16)

    @pl.loop(0, slots)
    def _(s):
        src = pl.multiple_of(order_ref[s] * passage, passage)
        dst = pl.multiple_of(s * passage, passage)
        keys = kv_ref[pl.ds(src, passage), :D]
        values = kv_ref[pl.ds(src, passage), D:]
        ks_ref[0, pl.ds(dst, passage)] = jnp.where(lower, keys, zero)
        ks_ref[1, pl.ds(dst, passage)] = jnp.where(lower, zero, keys)
        vs_ref[0, pl.ds(dst, passage)] = jnp.where(lower, values, zero)
        vs_ref[1, pl.ds(dst, passage)] = jnp.where(lower, zero, values)

    o_ref[...] = jnp.zeros_like(o_ref)
    aug_ref[...] = jnp.zeros_like(aug_ref)

    @pl.loop(0, item_ref[4, 0])
    def _(n):
        row0 = pl.multiple_of(item_ref[0, n] * CT, CT)
        key0 = pl.multiple_of(item_ref[1, n] * keys_q, keys_q)
        rows = lax.broadcasted_iota(jnp.int32, (CT, 1), 0)
        valid = (rows >= item_ref[2, n]) & (rows < item_ref[3, n])
        for pair in range(PAIRS):
            cols = slice(pair * LANES, (pair + 1) * LANES)
            q = q_ref[pl.ds(row0, CT), cols] * jnp.bfloat16(SCALE)
            outs, logs = [], []
            for head in range(2):
                scores = dot_nt(q, ks_ref[head, pl.ds(key0, keys_q), cols])
                top = jnp.max(scores, axis=1, keepdims=True)
                expo = jnp.exp(scores - top)
                total = jnp.sum(expo, axis=1, keepdims=True)
                outs.append(dot_nn(expo.astype(jnp.bfloat16), vs_ref[head, pl.ds(key0, keys_q), cols]) / total)
                logs.append(top + jnp.log(total))
            mixed = (outs[0] + outs[1]).astype(jnp.bfloat16)
            aug = triple_lanes(logs[0], logs[1], CT).astype(jnp.bfloat16)
            o_ref[pl.ds(row0, CT), cols] = jnp.where(valid, mixed, o_ref[pl.ds(row0, CT), cols])
            aug_ref[pl.ds(row0, CT), cols] = jnp.where(valid, aug, aug_ref[pl.ds(row0, CT), cols])


def smem_spec():
    return pl.BlockSpec(memory_space=pltpu.SMEM)


def vmem_spec():
    return pl.BlockSpec(memory_space=pltpu.VMEM)


def cross_forward(order, items, q, kv, passage):
    keys = kv.shape[0]
    return pl.pallas_call(
        partial(cross_forward_kernel, passage=passage),
        in_specs=[smem_spec(), smem_spec(), vmem_spec(), vmem_spec()],
        out_specs=[vmem_spec(), vmem_spec()],
        out_shape=[jax.ShapeDtypeStruct((LEN, D), jnp.bfloat16)] * 2,
        scratch_shapes=[pltpu.VMEM((2, keys, D), jnp.bfloat16)] * 2,
        compiler_params=pltpu.CompilerParams(vmem_limit_bytes=VMEM_LIMIT),
        cost_estimate=pl.CostEstimate(flops=2 * H * LEN * LEN * HD, bytes_accessed=10 * LEN * D, transcendentals=0),
    )(order, items, q, kv)


def cross_backward_kernel(order_ref, item_ref, q_ref, kv_ref, do_ref, o_ref, aug_ref,
                          dq_ref, dkv_ref, ks_ref, vs_ref, kt_ref, dk_ref, dv_ref, dqt_ref, passage):
    slots = order_ref.shape[0]
    per_q = slots // TARGETS
    keys_q = per_q * passage
    lane = lax.broadcasted_iota(jnp.int32, (passage, D), 1) % LANES
    lower = lane < HD
    ones = jnp.where((lane & (HD - 1)) < 3, 1.0, 0.0).astype(jnp.bfloat16)
    minus = -ones

    @pl.loop(0, slots)
    def _(s):
        src = pl.multiple_of(order_ref[s] * passage, passage)
        dst = pl.multiple_of(s * passage, passage)
        keys = kv_ref[pl.ds(src, passage), :D]
        values = kv_ref[pl.ds(src, passage), D:]
        ks_ref[0, pl.ds(dst, passage)] = jnp.where(lower, keys, minus)
        ks_ref[1, pl.ds(dst, passage)] = jnp.where(lower, minus, keys)
        vs_ref[0, pl.ds(dst, passage)] = jnp.where(lower, values, ones)
        vs_ref[1, pl.ds(dst, passage)] = jnp.where(lower, ones, values)

    lower_k = lax.broadcasted_iota(jnp.int32, (keys_q, LANES), 1) < HD
    for s in range(TARGETS):
        for pair in range(PAIRS):
            rows = slice(s * keys_q, (s + 1) * keys_q)
            cols = slice(pair * LANES, (pair + 1) * LANES)
            both = jnp.where(lower_k, ks_ref[0, rows, cols], ks_ref[1, rows, cols])
            kt_ref[cols, rows] = both.T
    dk_ref[...] = jnp.zeros_like(dk_ref)
    dv_ref[...] = jnp.zeros_like(dv_ref)
    dqt_ref[...] = jnp.zeros_like(dqt_ref)

    @pl.loop(0, item_ref[4, 0])
    def _(n):
        row0 = pl.multiple_of(item_ref[0, n] * CT, CT)
        key0 = pl.multiple_of(item_ref[1, n] * keys_q, keys_q)
        rows = lax.broadcasted_iota(jnp.int32, (CT, 1), 0)
        valid = (rows >= item_ref[2, n]) & (rows < item_ref[3, n])
        here = pl.ds(row0, CT)
        there = pl.ds(key0, keys_q)
        for pair in range(PAIRS):
            cols = slice(pair * LANES, (pair + 1) * LANES)
            q_scaled = q_ref[here, cols] * jnp.bfloat16(SCALE)
            do_pair = jnp.where(valid, do_ref[here, cols], jnp.zeros((), jnp.bfloat16))
            product = do_pair.astype(jnp.float32) * o_ref[here, cols].astype(jnp.float32)
            deltas = []
            for head in range(2):
                deltas.append(jnp.sum(jnp.where(in_half(CT, head), product, 0.0), axis=1, keepdims=True))
            aug_do = (-triple_lanes(deltas[0], deltas[1], CT)).astype(jnp.bfloat16)
            aug = jnp.where(valid, aug_ref[here, cols], jnp.bfloat16(1e30))
            parts = []
            for head in range(2):
                half = in_half(CT, head)
                q = jnp.where(half, q_scaled, aug)
                do = jnp.where(half, do_pair, aug_do)
                probs = jnp.exp(dot_nt(ks_ref[head, there, cols], q))
                grad_scores = probs * dot_nt(vs_ref[head, there, cols], do)
                ds = grad_scores.astype(jnp.bfloat16)
                parts.append((dot_nn(ds, q), dot_nn(probs.astype(jnp.bfloat16), do)))
                hrow = pair * LANES + head * HD
                dqt_ref[hrow : hrow + HD, here] += dot_nn(kt_ref[hrow : hrow + HD, there], ds)
            dk_ref[there, cols] += jnp.where(lower_k, parts[0][0], parts[1][0])
            dv_ref[there, cols] += jnp.where(lower_k, parts[0][1], parts[1][1])

    for pair in range(PAIRS):
        cols = slice(pair * LANES, (pair + 1) * LANES)
        dq_ref[:, cols] = (dqt_ref[cols, :] * SCALE).T.astype(jnp.bfloat16)

    @pl.loop(0, slots)
    def _(s):
        src = pl.multiple_of(s * passage, passage)
        dst = pl.multiple_of(order_ref[s] * passage, passage)
        dkv_ref[pl.ds(dst, passage), :D] = dk_ref[pl.ds(src, passage)].astype(jnp.bfloat16)
        dkv_ref[pl.ds(dst, passage), D:] = dv_ref[pl.ds(src, passage)].astype(jnp.bfloat16)


def cross_backward(order, items, q, kv, do, o, aug, passage):
    keys = kv.shape[0]
    return pl.pallas_call(
        partial(cross_backward_kernel, passage=passage),
        in_specs=[smem_spec(), smem_spec()] + [vmem_spec()] * 5,
        out_specs=[vmem_spec(), vmem_spec()],
        out_shape=[
            jax.ShapeDtypeStruct((LEN, D), jnp.bfloat16),
            jax.ShapeDtypeStruct((keys, 2 * D), jnp.bfloat16),
        ],
        scratch_shapes=[pltpu.VMEM((2, keys, D), jnp.bfloat16)] * 2
        + [
            pltpu.VMEM((D, keys), jnp.bfloat16),
            pltpu.VMEM((keys, D), jnp.float32),
            pltpu.VMEM((keys, D), jnp.float32),
            pltpu.VMEM((D, LEN), jnp.float32),
        ],
        compiler_params=pltpu.CompilerParams(vmem_limit_bytes=VMEM_LIMIT),
        cost_estimate=pl.CostEstimate(flops=5 * H * LEN * LEN * HD, bytes_accessed=18 * LEN * D, transcendentals=0),
    )(order, items, q, kv, do, o, aug)


def cross_items(lengths, questions):
    ends = jnp.cumsum(lengths)
    starts = ends - lengths
    tiles = LEN // CT
    slots = tiles + TARGETS - 1
    first = starts // CT
    last = (ends - 1) // CT
    count = last - first + 1
    done = jnp.cumsum(count)
    number = jnp.arange(slots, dtype=jnp.int32)
    seg = jnp.sum((number[:, None] >= done[None, :]).astype(jnp.int32), axis=1)
    pick = (jnp.minimum(seg, TARGETS - 1)[:, None] == jnp.arange(TARGETS, dtype=jnp.int32)[None, :]).astype(jnp.int32)
    take = lambda a: jnp.sum(pick * a[None, :], axis=1)
    tile = jnp.clip(take(first) + number - take(done - count), 0, tiles - 1)
    lo = jnp.clip(take(starts) - tile * CT, 0, CT)
    hi = jnp.clip(take(ends) - tile * CT, 0, CT)
    total = jnp.broadcast_to(jnp.sum(count), (slots,))
    return jnp.stack([tile, take(questions), lo, hi, total]).astype(jnp.int32)


def passage_order(passage_question):
    count = passage_question.shape[0]
    ids = jnp.arange(count, dtype=jnp.int32)
    before = (passage_question[None, :] < passage_question[:, None]) | (
        (passage_question[None, :] == passage_question[:, None]) & (ids[None, :] < ids[:, None])
    )
    rank = jnp.sum(before.astype(jnp.int32), axis=1)
    return jnp.sum(jnp.where(rank[:, None] == ids[None, :], ids[:, None], 0), axis=0).astype(jnp.int32)


def segment_aug(segment):
    place = jnp.arange(LANES, dtype=jnp.int32)[None, :] & (HD - 1)
    seg = segment[:, None]
    mark = (place >= 3) & (place < 3 + TARGETS)
    same = place - 3 == seg
    aq = jnp.where(mark & same, 1.0, 0.0).astype(jnp.bfloat16)
    ak = jnp.where(place < 3, -1.0, jnp.where(mark & ~same, NEG, 0.0)).astype(jnp.bfloat16)
    av = jnp.broadcast_to(jnp.where(place < 3, 1.0, 0.0), (LEN, LANES)).astype(jnp.bfloat16)
    return aq, ak, av


ROWS = 256


def norm_parts(values):
    return lax.rsqrt(jnp.mean(values * values, axis=1, keepdims=True) + eps_norm)


def norm_back(values, inverse, gain, grad):
    scaled = grad * gain
    inner = jnp.mean(scaled * values, axis=1, keepdims=True)
    return inverse * scaled - values * (inverse * inverse * inverse * inner)


def bits_of(count):
    return count.bit_length() - 1


def place_bits(n_blk, n_dp, kind):
    blk = [("blk", bit) for bit in range(bits_of(n_blk))]
    dp = [("dp", bit) for bit in range(bits_of(n_dp))]
    if kind == "x":
        return blk[:1] + dp + blk[1:]
    if kind == "z":
        return blk[:1] + blk[2:] + blk[1:2]
    return blk


def position(owner, piece, order):
    slot = 0
    for axis, bit in order:
        mine = (lax.axis_index(axis) // (1 << bit)) % 2
        static = ((owner if axis == "blk" else piece) >> bit) & 1
        slot = 2 * slot + (1 - mine if static else mine)
    return slot


def partner(axis, bit):
    me = lax.axis_index(axis)
    mine = (me // (1 << bit)) % 2
    return {axis: me + (1 - 2 * mine) * (1 << bit)}


class Exchange:
    def __init__(self, count, n_blk, n_dp, kind):
        if kind == "x" and count % n_dp:
            kind = "y"
        self.n_blk, self.n_dp, self.count, self.kind = n_blk, n_dp, count, kind
        self.order = place_bits(n_blk, n_dp, kind)
        self.pieces = n_dp if kind == "x" else 1
        self.slots = n_blk * self.pieces
        self.mats = count // self.pieces
        self.last = [("dp", bit) for bit in range(bits_of(n_dp))]
        self.steps = len(self.order) + len(self.last)
        self.rows = D // n_blk
        self.offsets = []
        at = 0
        for k in range(len(self.order)):
            size = self.slots >> (k + 1)
            self.offsets.append((at, size))
            at += size
        for j in range(len(self.last)):
            size = (1 << j) if kind == "x" else 1
            self.offsets.append((at, size))
            at += size
        self.received = at

    def scratch(self):
        shape = (self.mats, self.rows, D)
        return [
            pltpu.VMEM((self.slots,) + shape, jnp.bfloat16),
            pltpu.VMEM((self.received,) + shape, jnp.bfloat16),
            pltpu.SemaphoreType.DMA((self.steps,)),
            pltpu.SemaphoreType.DMA((self.steps,)),
        ]

    def bind(self, refs, out_ref):
        self.buf, self.recv, self.send_sem, self.recv_sem = refs
        self.out = out_ref

    def put(self, index, value):
        piece, inner = index // self.mats, index % self.mats
        for owner in range(self.n_blk):
            slot = position(owner, piece, self.order)
            self.buf[slot, inner] = value[owner * self.rows : (owner + 1) * self.rows].astype(jnp.bfloat16)

    def copy(self, k):
        at, size = self.offsets[k]
        if k < len(self.order):
            axis, bit = self.order[k]
            src = self.buf.at[pl.ds(size, size)]
        else:
            axis, bit = self.last[k - len(self.order)]
            src = self.buf.at[pl.ds(0, size)]
        return pltpu.make_async_remote_copy(
            src_ref=src,
            dst_ref=self.recv.at[pl.ds(at, size)],
            send_sem=self.send_sem.at[k],
            recv_sem=self.recv_sem.at[k],
            device_id=partner(axis, bit),
            device_id_type=pl.DeviceIdType.MESH,
        )

    def start(self, k):
        self.copy(k).start()

    def finish(self, k):
        self.copy(k).wait()
        at, size = self.offsets[k]
        final = k == self.steps - 1
        if k < len(self.order) or self.kind != "x":
            for s in range(size):
                for m in range(self.mats):
                    total = self.buf[s, m].astype(jnp.float32) + self.recv[at + s, m].astype(jnp.float32)
                    if final:
                        self.out[m] = total
                    else:
                        self.buf[s, m] = total.astype(jnp.bfloat16)
            return
        for s in range(size):
            for m in range(self.mats):
                self.buf[size + s, m] = self.recv[at + s, m]
        if final:
            for s in range(self.pieces):
                spot = position(0, s, self.last[::-1])
                for m in range(self.mats):
                    self.out[spot * self.mats + m] = self.buf[s, m].astype(jnp.float32)

    def advance(self, k):
        self.finish(k)
        if k + 1 < self.steps:
            self.start(k + 1)


def enter_barrier(n_blk, n_dp):
    barrier = pltpu.get_barrier_semaphore()
    links = [("blk", bit) for bit in range(bits_of(n_blk))] + [("dp", bit) for bit in range(bits_of(n_dp))]
    for axis, bit in links:
        pl.semaphore_signal(barrier, inc=1, device_id=partner(axis, bit), device_id_type=pl.DeviceIdType.MESH)
    pl.semaphore_wait(barrier, len(links))


def tail_kernel(n_blk, n_dp, plans, *refs):
    (x_ref, gain_ref, dy1_ref, act_ref, dq_ref, dk_ref, dv_ref, wq_ref, wk_ref, wv_ref,
     actc_ref, dqc_ref, enc_ref, dkv_ref, o_ref, oc_ref, e2_ref, small_ref) = refs[:18]
    outs = refs[18 : 18 + len(plans)]
    dx_ref, sums_ref = refs[18 + len(plans) : 20 + len(plans)]
    scratch = refs[20 + len(plans) :]
    for i, plan in enumerate(plans):
        plan.bind(scratch[4 * i : 4 * i + 4], outs[i])
    tot_ref, got_ref, tsend, trecv = scratch[4 * len(plans) :]
    enter_barrier(n_blk, n_dp)
    crossx, crossy, selfx, selfy = plans

    crossx.put(0, dot_tn(actc_ref[...], dqc_ref[...]))
    crossx.put(1, dot_tn(enc_ref[...], dkv_ref[:, :D]))
    crossx.start(0)
    crossy.put(0, dot_tn(enc_ref[...], dkv_ref[:, D:]))
    crossy.put(1, dot_tn(oc_ref[...], e2_ref[...]))
    crossy.put(2, dot_tn(o_ref[...], dy1_ref[...].astype(jnp.bfloat16)))
    crossy.start(0)
    crossx.advance(0)
    selfx.put(0, dot_tn(act_ref[...], dq_ref[...]))
    selfx.put(1, dot_tn(act_ref[...], dk_ref[...]))
    selfx.start(0)
    crossy.advance(0)
    selfy.put(0, dot_tn(act_ref[...], dv_ref[...]))
    selfy.start(0)
    selfx.advance(0)
    gain_sum = jnp.zeros((1, D), jnp.float32)
    for i, r in enumerate(range(0, LEN, ROWS)):
        rows = slice(r, r + ROWS)
        da = dot_nt(dq_ref[rows], wq_ref[...]) + dot_nt(dk_ref[rows], wk_ref[...]) + dot_nt(dv_ref[rows], wv_ref[...])
        x = x_ref[rows].astype(jnp.float32)
        inverse = norm_parts(x)
        gain_sum = gain_sum + jnp.sum(da * x * inverse, axis=0, keepdims=True)
        dx_ref[rows] = dy1_ref[rows] + norm_back(x, inverse, gain_ref[...], da)
        if i == 0:
            selfy.advance(0)
        if i == 1:
            crossx.advance(1)
        if i == 2:
            crossy.advance(1)
    tot_ref[...] = small_ref[...]
    tot_ref[0:1] = gain_sum
    links = [("blk", bit) for bit in range(bits_of(n_blk))] + [("dp", bit) for bit in range(bits_of(n_dp))]

    def small_copy(j):
        axis, bit = links[j]
        return pltpu.make_async_remote_copy(
            src_ref=tot_ref,
            dst_ref=got_ref.at[j],
            send_sem=tsend.at[j],
            recv_sem=trecv.at[j],
            device_id=partner(axis, bit),
            device_id_type=pl.DeviceIdType.MESH,
        )

    small_copy(0).start()
    longest = max(plan.steps for plan in plans)
    for k in range(1, longest):
        for plan in (selfx, selfy, crossx, crossy):
            step = k if plan in (selfx, selfy) else k + 1
            if step < plan.steps:
                plan.advance(step)
        if k - 1 < len(links):
            small_copy(k - 1).wait()
            tot_ref[...] = tot_ref[...] + got_ref[k - 1]
            if k < len(links):
                small_copy(k).start()
    for j in range(longest - 1, len(links)):
        small_copy(j).wait()
        tot_ref[...] = tot_ref[...] + got_ref[j]
        if j + 1 < len(links):
            small_copy(j + 1).start()
    sums_ref[...] = tot_ref[...]


def tail_block(n_blk, n_dp, *args):
    plans = [
        Exchange(2, n_blk, n_dp, "x"),
        Exchange(3, n_blk, n_dp, "y"),
        Exchange(2, n_blk, n_dp, "x"),
        Exchange(1, n_blk, n_dp, "y"),
    ]
    links = bits_of(n_blk) + bits_of(n_dp)
    scratch = [item for plan in plans for item in plan.scratch()]
    scratch += [
        pltpu.VMEM((8, D), jnp.float32),
        pltpu.VMEM((links, 8, D), jnp.float32),
        pltpu.SemaphoreType.DMA((links,)),
        pltpu.SemaphoreType.DMA((links,)),
    ]
    return pl.pallas_call(
        partial(tail_kernel, n_blk, n_dp, plans),
        in_specs=[vmem_spec()] * len(args),
        out_specs=[vmem_spec()] * (len(plans) + 2),
        out_shape=[jax.ShapeDtypeStruct((plan.count, plan.rows, D), jnp.float32) for plan in plans]
        + [jax.ShapeDtypeStruct((LEN, D), jnp.float32), jax.ShapeDtypeStruct((8, D), jnp.float32)],
        scratch_shapes=scratch,
        compiler_params=pltpu.CompilerParams(
            vmem_limit_bytes=VMEM_LIMIT, collective_id=1, has_side_effects=True
        ),
        cost_estimate=pl.CostEstimate(flops=22 * LEN * D * D, bytes_accessed=80 * LEN * D, transcendentals=0),
    )(*args)


FF_STEPS = 4


def normal_cdf_pair(u):
    x = jnp.abs(u) * 0.7071067811865476
    gauss = jnp.exp(-0.5 * u * u)
    t = 1.0 / (1.0 + 0.3275911 * x)
    poly = ((((1.061405429 * t - 1.453152027) * t + 1.421413741) * t - 0.284496736) * t + 0.254829592) * t
    tail = 0.5 * poly * gauss
    return jnp.where(u >= 0, 1.0 - tail, tail), gauss * 0.3989422804014327


def rest_slot(owner, piece, order):
    slot = 0
    for axis, bit in order[1:]:
        mine = (lax.axis_index(axis) // (1 << bit)) % 2
        its = ((owner if axis == "blk" else piece) // (1 << bit)) % 2
        slot = 2 * slot + (its + mine) % 2
    return slot


def feed_kernel(plan_in, plan_out, y1_ref, oc_ref, wco_ref, gain_ref, g_ref, w1_ref, w2_ref,
                out_ref, isend_ref, ikeep_ref, osend_ref, okeep_ref, dy2_ref, e2_ref, doc_ref, dgain_ref,
                y2_ref, act_ref, acc_ref, da_ref, hid_ref, du_ref):
    step = pl.program_id(0)
    even_core = lax.axis_index("blk") % 2 == 0

    @pl.when(step == 0)
    def _():
        for r in range(0, LEN, ROWS):
            rows = slice(r, r + ROWS)
            y2 = y1_ref[rows] + dot_nn(oc_ref[rows], wco_ref[...])
            y2_ref[rows] = y2
            act_ref[rows] = (y2 * norm_parts(y2) * gain_ref[...]).astype(jnp.bfloat16)
        acc_ref[...] = y2_ref[...]
        da_ref[...] = jnp.zeros_like(da_ref)

    for r in range(0, LEN, ROWS):
        rows = slice(r, r + ROWS)
        u = dot_nn(act_ref[rows], w1_ref[...])
        dh = dot_nt(g_ref[rows], w2_ref[...])
        cdf, density = normal_cdf_pair(u)
        hid = (u * cdf).astype(jnp.bfloat16)
        du = (dh * (cdf + u * density)).astype(jnp.bfloat16)
        hid_ref[rows] = hid
        du_ref[rows] = du
        acc_ref[rows] += dot_nn(hid, w2_ref[...])
        da_ref[rows] += dot_nt(du, w1_ref[...])

    dw2 = dot_tn(hid_ref[...], g_ref[...])
    own_rows = plan_out.rows * plan_out.count
    group = dw2.shape[0] // own_rows
    for t in range(0, group, 2):
        for m in range(plan_out.count):
            piece, inner = m // plan_out.mats, m % plan_out.mats
            even = dw2[t * own_rows + m * plan_out.rows : t * own_rows + (m + 1) * plan_out.rows]
            odd = dw2[(t + 1) * own_rows + m * plan_out.rows : (t + 1) * own_rows + (m + 1) * plan_out.rows]
            slot = rest_slot(step * group + t, piece, plan_out.order)
            osend_ref[slot, inner] = jnp.where(even_core, odd, even).astype(jnp.bfloat16)
            okeep_ref[slot, inner] = jnp.where(even_core, even, odd).astype(jnp.bfloat16)
    dw1 = dot_tn(act_ref[...], du_ref[...])
    for t in range(0, plan_in.n_blk, 2):
        even = dw1[t * plan_in.rows : (t + 1) * plan_in.rows]
        odd = dw1[(t + 1) * plan_in.rows : (t + 2) * plan_in.rows]
        slot = rest_slot(t, 0, plan_in.order)
        isend_ref[slot, 0] = jnp.where(even_core, odd, even).astype(jnp.bfloat16)
        ikeep_ref[slot, 0] = jnp.where(even_core, even, odd).astype(jnp.bfloat16)

    @pl.when(step == FF_STEPS - 1)
    def _():
        gain_sum = jnp.zeros((1, D), jnp.float32)
        for r in range(0, LEN, ROWS):
            rows = slice(r, r + ROWS)
            out_ref[rows] = acc_ref[rows].astype(jnp.bfloat16)
            y2 = y2_ref[rows]
            inverse = norm_parts(y2)
            da = da_ref[rows]
            gain_sum = gain_sum + jnp.sum(da * y2 * inverse, axis=0, keepdims=True)
            dy2 = g_ref[rows].astype(jnp.float32) + norm_back(y2, inverse, gain_ref[...], da)
            dy2_ref[rows] = dy2
            e2 = dy2.astype(jnp.bfloat16)
            e2_ref[rows] = e2
            doc_ref[rows] = dot_nt(e2, wco_ref[...]).astype(jnp.bfloat16)
        dgain_ref[...] = gain_sum


def feed_block(y1, oc, wco, gain, g, w1, w2, plan_in, plan_out):
    ff = w1.shape[1]
    cols = ff // FF_STEPS
    fixed = lambda shape: pl.BlockSpec(shape, lambda c: (0,) * len(shape))
    half_in = (plan_in.slots // 2, plan_in.mats, plan_in.rows, D)
    half_out = (plan_out.slots // 2, plan_out.mats, plan_out.rows, D)
    in_spec = pl.BlockSpec((half_in[0], 1) + half_in[2:], lambda c: (0, c, 0, 0))
    like = jax.ShapeDtypeStruct
    return pl.pallas_call(
        partial(feed_kernel, plan_in, plan_out),
        grid=(FF_STEPS,),
        in_specs=[
            fixed((LEN, D)), fixed((LEN, D)), fixed((D, D)), fixed((1, D)), fixed((LEN, D)),
            pl.BlockSpec((D, cols), lambda c: (0, c)),
            pl.BlockSpec((cols, D), lambda c: (c, 0)),
        ],
        out_specs=[
            fixed((LEN, D)), in_spec, in_spec, fixed(half_out), fixed(half_out),
            fixed((LEN, D)), fixed((LEN, D)), fixed((LEN, D)), fixed((1, D)),
        ],
        out_shape=[
            like((LEN, D), jnp.bfloat16),
            like(half_in, jnp.bfloat16),
            like(half_in, jnp.bfloat16),
            like(half_out, jnp.bfloat16),
            like(half_out, jnp.bfloat16),
            like((LEN, D), jnp.float32),
            like((LEN, D), jnp.bfloat16),
            like((LEN, D), jnp.bfloat16),
            like((1, D), jnp.float32),
        ],
        scratch_shapes=[
            pltpu.VMEM((LEN, D), jnp.float32),
            pltpu.VMEM((LEN, D), jnp.bfloat16),
            pltpu.VMEM((LEN, D), jnp.float32),
            pltpu.VMEM((LEN, D), jnp.float32),
            pltpu.VMEM((LEN, cols), jnp.bfloat16),
            pltpu.VMEM((LEN, cols), jnp.bfloat16),
        ],
        compiler_params=pltpu.CompilerParams(vmem_limit_bytes=VMEM_LIMIT),
        cost_estimate=pl.CostEstimate(flops=12 * LEN * D * ff, bytes_accessed=40 * LEN * D, transcendentals=0),
    )(y1, oc, wco, gain, g, w1, w2)


def swap(value, axis, bit, size):
    return lax.ppermute(value, axis, [(i, i ^ (1 << bit)) for i in range(size)])


def total_of(terms):
    out = terms[0].astype(jnp.float32)
    for term in terms[1:]:
        out = out + term.astype(jnp.float32)
    return out


def gather_rows(rows, n_blk):
    out = rows
    masks = [0]
    for bit in reversed(range(bits_of(n_blk))):
        out = jnp.concatenate([out, swap(out, "blk", bit, n_blk)], axis=0)
        masks = masks + [mask | (1 << bit) for mask in masks]
    return out, masks


def scatter_slots(value, n_blk):
    terms = [value]
    for bit in range(bits_of(n_blk)):
        half = terms[0].shape[0] // 2
        send = total_of([t[half:] for t in terms]).astype(jnp.bfloat16)
        kept = total_of([t[:half] for t in terms]).astype(jnp.bfloat16)
        terms = [kept, swap(send, "blk", bit, n_blk)]
    return total_of(terms)[0]


def scatter_step(terms, axis, bit, n):
    half = terms[0].shape[0] // 2
    send = total_of([t[half:] for t in terms]).astype(jnp.bfloat16)
    kept = total_of([t[:half] for t in terms]).astype(jnp.bfloat16)
    return [kept, swap(send, axis, bit, n)]


def per_device(
    decoder_rows,
    encoder_rows,
    target_lengths,
    target_question,
    passage_question,
    self_gain,
    self_query,
    self_key,
    self_value,
    self_output,
    position_bias_matrix,
    cross_gain,
    cross_query,
    cross_key,
    cross_value,
    cross_output,
    feed_gain,
    feed_input_weight,
    feed_out,
    cotangent,
    n_dp,
    n_blk,
):
    passage = encoder_rows.shape[0]
    sizes = {"blk": n_blk, "dp": n_dp}
    me = lax.axis_index("blk")
    encoder_all, masks = gather_rows(encoder_rows, n_blk)
    slot_device = me ^ jnp.array(masks, dtype=jnp.int32)
    slot_pick = slot_device[:, None] == jnp.arange(n_blk, dtype=jnp.int32)[None, :]
    slot_question = jnp.sum(jnp.where(slot_pick, passage_question[None, :], 0), axis=1)
    order = passage_order(slot_question)
    items = cross_items(target_lengths[0], target_question[0])
    positions = jnp.arange(LEN, dtype=jnp.int32)
    seg_ends = jnp.cumsum(target_lengths[0])
    segment = jnp.sum((positions[:, None] >= seg_ends[None, : TARGETS - 1]).astype(jnp.int32), axis=-1)
    aq, ak, av = segment_aug(segment)
    table_pairs = position_bias_matrix.T.reshape(PAIRS, 2, BUCKETS)
    self_gain2, cross_gain2, feed_gain2 = self_gain[None], cross_gain[None], feed_gain[None]

    inputs = decoder_rows.astype(jnp.float32)
    act_self = (inputs * norm_parts(inputs) * self_gain2).astype(jnp.bfloat16)
    query_self = dot_nn(act_self, self_query).astype(jnp.bfloat16)
    key_self = dot_nn(act_self, self_key).astype(jnp.bfloat16)
    value_self = dot_nn(act_self, self_value).astype(jnp.bfloat16)
    attn_self, aug_self = self_forward(query_self, key_self, value_self, aq, ak, table_pairs)
    attn_self, encoder_all = lax.optimization_barrier((attn_self, encoder_all))
    resid_self = inputs + dot_nn(attn_self, self_output)
    inv_cross = norm_parts(resid_self)
    act_cross = (resid_self * inv_cross * cross_gain2).astype(jnp.bfloat16)
    query_cross = dot_nn(act_cross, cross_query).astype(jnp.bfloat16)
    pair_weight = jnp.concatenate([cross_key, cross_value], axis=1)
    pair_all = dot_nn(encoder_all, pair_weight).astype(jnp.bfloat16)
    attn_cross, aug_cross = cross_forward(order, items, query_cross, pair_all, passage)

    plan_in = Exchange(4, n_blk, n_dp, "y")
    plan_out = Exchange(4, n_blk, n_dp, "x")
    (block_out, in_send, in_keep, out_send, out_keep, grad_resid_cross, round_cross, grad_attn_cross, gain_feed) = feed_block(
        resid_self, attn_cross, cross_output, feed_gain2, cotangent, feed_input_weight, feed_out, plan_in, plan_out
    )
    first_in, first_out = plan_in.order[0], plan_out.order[0]
    terms_in = [in_keep, swap(in_send, *first_in, sizes[first_in[0]])]
    terms_out = [out_keep, swap(out_send, *first_out, sizes[first_out[0]])]
    (terms_in, terms_out), grad_attn_cross = lax.optimization_barrier(((terms_in, terms_out), grad_attn_cross))
    step = lambda plan, terms, k: scatter_step(terms, *plan.order[k], sizes[plan.order[k][0]])
    next_in, next_out = step(plan_in, terms_in, 1), step(plan_out, terms_out, 1)
    dqc, dkv = cross_backward(
        order, items, query_cross, pair_all, grad_attn_cross, attn_cross, aug_cross, passage
    )
    (terms_in, terms_out), dqc, dkv = lax.optimization_barrier(((next_in, next_out), dqc, dkv))
    next_in, next_out = step(plan_in, terms_in, 2), step(plan_out, terms_out, 2)
    encoder_part = dot_nt(dkv, pair_weight).astype(jnp.bfloat16)
    da_cross = dot_nt(dqc, cross_query)
    gain_cross = jnp.sum(da_cross * resid_self * inv_cross, axis=0)
    grad_resid_self = grad_resid_cross + norm_back(resid_self, inv_cross, cross_gain2, da_cross)
    round_self = grad_resid_self.astype(jnp.bfloat16)
    grad_attn_self = dot_nt(round_self, self_output).astype(jnp.bfloat16)
    (terms_in, terms_out), grad_attn_self, encoder_part = lax.optimization_barrier(
        ((next_in, next_out), grad_attn_self, encoder_part)
    )
    for k in range(3, len(plan_in.order)):
        terms_in = step(plan_in, terms_in, k)
    for k in range(3, len(plan_out.order)):
        terms_out = step(plan_out, terms_out, k)
    total_in = total_of(terms_in)[0]
    for bit in range(bits_of(n_dp)):
        own = total_in.astype(jnp.bfloat16)
        total_in = total_of([own, swap(own, "dp", bit, n_dp)])
    sum_feed_in = jnp.swapaxes(total_in, 0, 1).reshape(D // n_blk, -1)
    total_out = total_of(terms_out)[0]
    if plan_out.kind == "x":
        for bit in range(bits_of(n_dp)):
            own = total_out.astype(jnp.bfloat16)
            other = swap(own, "dp", bit, n_dp)
            low = (lax.axis_index("dp") >> bit) & 1 == 0
            total_out = jnp.concatenate([jnp.where(low, own, other), jnp.where(low, other, own)], axis=0)
        total_out = total_out.astype(jnp.float32)
    else:
        for bit in range(bits_of(n_dp)):
            own = total_out.astype(jnp.bfloat16)
            total_out = total_of([own, swap(own, "dp", bit, n_dp)])
    sum_feed_out = total_out.reshape(-1, D)
    grad_encoder = scatter_slots(encoder_part.reshape(n_blk, passage, D), n_blk)
    dq, dk, dv, table_parts = self_backward(
        query_self, key_self, value_self, grad_attn_self, attn_self, aug_self, ak, av, table_pairs
    )
    sum_feed_in, sum_feed_out, grad_encoder, dq, dk, dv = lax.optimization_barrier(
        (sum_feed_in, sum_feed_out, grad_encoder, dq, dk, dv)
    )
    small = jnp.concatenate(
        [
            jnp.zeros((1, D), jnp.float32),
            gain_cross[None],
            gain_feed,
            jnp.pad(table_parts.reshape(1, H * BUCKETS), ((0, 0), (0, D - H * BUCKETS))),
            jnp.zeros((4, D), jnp.float32),
        ],
        axis=0,
    )
    crossx, crossy, selfx, selfy, grad_decoder, sums = tail_block(
        n_blk, n_dp,
        decoder_rows, self_gain2, grad_resid_self, act_self, dq, dk, dv, self_query, self_key, self_value,
        act_cross, dqc, encoder_all, dkv, attn_self, attn_cross, round_cross, small,
    )
    return (
        block_out,
        grad_decoder,
        grad_encoder,
        sums[0],
        selfx[0],
        selfx[1],
        selfy[0],
        crossy[2],
        sums[3, : H * BUCKETS].reshape(H, BUCKETS).T,
        sums[1],
        crossx[0],
        crossx[1],
        crossy[0],
        crossy[1],
        sums[2],
        sum_feed_in,
        sum_feed_out,
    )


def solution(mesh):
    split, copied, owned = P(("dp", "blk"), None), P(), P("blk", None)
    return jax.shard_map(
        partial(per_device, n_dp=mesh.shape["dp"], n_blk=mesh.shape["blk"]),
        mesh=mesh,
        in_specs=(split,) * 4 + (P("dp"),) + (copied,) * 14 + (split,),
        out_specs=(split,) * 3 + (copied,) + (owned,) * 4 + (copied,) * 2 + (owned,) * 4 + (copied,) + (owned,) * 2,
        check_vma=False,
    )
```

profile of v0, /device:TPU:0, one launch (start us, length us, event | category | flops | bytes accessed | tf_op | source)
XLA Modules:
  0.0 388.7 jit_solution(12309938617186344194)
XLA Ops:
  0.7 4.1 %collective-permute-start = (bf16[64,768]{1,0:T(8,128)(2,1)}, bf16[64,768]{1,0:T(8,128)(2,1)S(1)}, u32[]{:S(2)}, u32[]{:S(2)}) collective-permute-start(bf16[64,768]{1,0:T(8,128)(2,1)} %param.22), channel_id=1, source_target_pairs={{0,8},{1,9},{2,10},{3,11},{4,12},{5,13},{6,14},{7,15},{8,0},{9,1},... | collective-permute-start | bytes 294920 | tf_op jit(solution)/shard_map/ppermute | solution.py:827
  4.8 1.6 constant_dynamic-update-slice_fusion.4
  6.4 0.8 reduce-window.6
  7.9 1.8 fusion
  10.1 0.8 copy-done.35
  11.0 2.6 convolution_convert_fusion.6.q_ref
  13.6 2.5 convolution_convert_fusion.5.k_ref
  17.0 2.4 constant_dynamic-update-slice_fusion.6
  20.0 1.1 select_convert_fusion
  21.7 1.6 collective-permute-start.1
  23.8 4.3 %collective-permute-done.1 = bf16[128,768]{1,0:T(8,128)(2,1)S(1)} collective-permute-done((bf16[128,768]{1,0:T(8,128)(2,1)S(1)}, bf16[128,768]{1,0:T(8,128)(2,1)S(1)}, u32[]{:S(2)}, u32[]{:S(2)}) %collective-permute-start.1) | collective-permute-done | bytes 196640 | tf_op jit(solution)/shard_map/ppermute | solution.py:827
  28.9 1.5 collective-permute-start.2
  32.9 1.3 stack.10.item_ref
  34.2 4.5 %convolution_convert_fusion.4.v_ref = bf16[1024,768]{1,0:T(8,128)(2,1)} fusion(bf16[1024,768]{1,0:T(8,128)(2,1)} %copy-done.9, bf16[768,768]{1,0:T(8,128)(2,1)} %refs_9_.1), kind=kOutput, calls=%fused_computation.19 | convolution fusion | flops 1208745984 | bytes 4325376 | tf_op jit(solution)/shard_map/dot_general | solution.py:29
  38.8 0.9 pad_maximum_fusion
  40.3 1.4 copy-done.14
  41.7 24.7 %shard_map.332 = (bf16[1024,768]{1,0:T(8,128)(2,1)}, bf16[1024,768]{1,0:T(8,128)(2,1)}) custom-call(bf16[1024,768]{1,0:T(8,128)(2,1)} %convolution_convert_fusion.6.q_ref, bf16[1024,768]{1,0:T(8,128)(2,1)} %convolution_convert_fusion.5.k_ref, bf16[1024,768]{1,0:T(8,128)(2,1)} %convolution_convert_fusion.4.v_ref, ...), custom_call_target="tpu_custom_call" | custom-call | flops 3221225472 | bytes 7864320 | tf_op jit(solution)/shard_map/pallas_call | solution.py:131
  68.5 2.1 constant_dynamic-update-slice_fusion.refs_12_
  70.6 1.5 multiply_reduce_fusion.2
  72.5 1.3 copy-done.1
  73.8 2.5 convolution_convert_fusion.3.q_ref
  77.1 4.1 %convolution_convert_fusion.kv_ref = bf16[1024,1536]{1,0:T(8,128)(2,1)} fusion(bf16[1024,768]{1,0:T(8,128)(2,1)S(1)} %copy-done.23, bf16[768,1536]{1,0:T(8,128)(2,1)S(1)} %copy-done.15), kind=kOutput, calls=%fused_computation.3 | convolution fusion | flops 2417491968 | bytes 7077888 | tf_op jit(solution)/shard_map/dot_general | solution.py:29
  81.1 16.8 %shard_map.333 = (bf16[1024,768]{1,0:T(8,128)(2,1)}, bf16[1024,768]{1,0:T(8,128)(2,1)}) custom-call(s32[16]{0:T(128)} %select_reduce_fusion.order_ref, s32[5,7]{1,0:T(8,128)} %stack.10.item_ref, bf16[1024,768]{1,0:T(8,128)(2,1)} %convolution_convert_fusion.3.q_ref, bf16[1024,1536]{1,0:T(8,128)(2,1)} %convolution_convert_fusion.kv_ref), custom_call_target="tpu_custom_call" | custom-call | flops 1610612736 | bytes 7864320 | tf_op jit(solution)/shard_map/pallas_call | solution.py:300
  98.0 50.5 %shard_map.334 = (bf16[1024,768]{1,0:T(8,128)(2,1)}, bf16[8,4,48,768]{3,2,1,0:T(8,128)(2,1)}, bf16[8,4,48,768]{3,2,1,0:T(8,128)(2,1)}, bf16[16,2,48,768]{3,2,1,0...) custom-call(f32[1024,768]{1,0:T(8,128)} %copy-done.1, ...), custom_call_target="tpu_custom_call" | custom-call | flops 28991029248 | bytes 31457280 | tf_op jit(solution)/shard_map/pallas_call | solution.py:790
  149.1 4.2 %collective-permute-done.4 = bf16[8,4,48,768]{3,2,1,0:T(8,128)(2,1)S(1)} collective-permute-done((bf16[8,4,48,768]{3,2,1,0:T(8,128)(2,1)}, bf16[8,4,48,768]{3,2,1,0:T(8,128)(2,1)S(1)}, u32[]{:S(2)}, u32[]{:S(2)}) %collective-permute-start.4) | collective-permute-done | bytes 2359328 | tf_op jit(solution)/shard_map/ppermute | solution.py:827
  153.3 3.4 collective-permute-done.5
  156.7 3.4 add_convert_fusion.2
  160.1 3.2 collective-permute-start.6
  163.3 1.7 add_convert_fusion
  165.0 1.3 collective-permute-start.7
  166.9 27.2 %shard_map.335 = (bf16[1024,768]{1,0:T(8,128)(2,1)}, bf16[1024,1536]{1,0:T(8,128)(2,1)}) custom-call(s32[16]{0:T(128)} %select_reduce_fusion.order_ref, s32[5,7]{1,0:T(8,128)} %stack.10.item_ref, bf16[1024,768]{1,0:T(8,128)(2,1)} %convolution_convert_fusion.3.q_ref, bf16[1024,1536]{1,0:T(8,128)(2,1)} %convolution_convert_fusion.kv_ref, ...), custom_call_target="tpu_custom_call" | custom-call | flops 4026531840 | bytes 14155776 | tf_op jit(solution)/shard_map/pallas_call | solution.py:389
  194.1 4.1 %multiply_reduce_fusion = (f32[768]{0:T(1024)S(1)}, f32[1024]{0:T(1024)S(1)}, f32[1024,768]{1,0:T(8,128)S(1)}) fusion(f32[1024,768]{1,0:T(8,128)} %copy-done.1, f32[1024]{0:T(1024)S(1)} %add_rsqrt_fusion, f32[768]{0:T(1024)S(1)} %copy-done.21, bf16[1024,768]{1,0:T(8,128)(2,1)} %get-tuple-element.86.refs_11_, bf16[768,768]{1,0:T(8,128)(2,1)S(1)} %copy-done), kind=kOutput, calls=%fused_computation.7 | convolution fusion | flops 1212676352 | bytes 9058304 | tf_op jit(solution)/shard_map/dot_general | solution.py:33
  198.3 1.7 add_convert_fusion.6
  200.0 4.8 %collective-permute-start.8 = (bf16[2,4,48,768]{3,2,1,0:T(8,128)(2,1)S(1)}, bf16[2,4,48,768]{3,2,1,0:T(8,128)(2,1)S(1)}, u32[]{:S(2)}, u32[]{:S(2)}) collective-permute-start(bf16[2,4,48,768]{3,2,1,0:T(8,128)(2,1)S(1)} %get-tuple-element.137), channel_id=1, source_target_pairs={{0,4},{1,5},{2,6},{3,7},{4,0},{5,1},{6,2},{7,3},{8,12},{9,13},{10,... | collective-permute-start | bytes 1769480 | tf_op jit(solution)/shard_map/ppermute | solution.py:827
  204.7 1.5 add_convert_fusion.4
  206.2 1.1 collective-permute-start.9
  208.6 2.6 convolution_convert_fusion.2.do_ref
  212.0 0.9 copy-done.40
  212.9 2.6 convolution_convert_fusion.1
  215.6 2.3 collective-permute-done.8
  217.8 3.0 collective-permute-done.9
  221.0 0.9 add_convert_fusion.9
  221.9 0.9 collective-permute-start.12
  222.8 0.9 slice.199
  224.5 27.7 %shard_map.336 = (bf16[1024,768]{1,0:T(8,128)(2,1)}, bf16[1024,768]{1,0:T(8,128)(2,1)}, bf16[1024,768]{1,0:T(8,128)(2,1)}, f32[6,2,32]{2,1,0:T(2,128)}) custom-call(bf16[1024,768]{1,0:T(8,128)(2,1)} %convolution_convert_fusion.6.q_ref, bf16[1024,768]{1,0:T(8,128)(2,1)} %convolution_convert_fusion.5.k_ref, bf16[1024,768]{1,0:T(8,128)(2,1)} %convolution_convert_fusion.4.v_ref, ...), custom_call_target="tpu_custom_call" | custom-call | flops 8053063680 | bytes 14155776 | tf_op jit(solution)/shard_map/pallas_call | solution.py:224
  253.7 0.9 add_convert_fusion.16
  254.6 2.6 collective-permute-start.13
  257.3 7.7 %collective-permute-done.13 = bf16[1,2,48,768]{3,2,1,0:T(8,128)(2,1)S(1)} collective-permute-done((bf16[1,2,48,768]{3,2,1,0:T(8,128)(2,1)S(1)}, bf16[1,2,48,768]{3,2,1,0:T(8,128)(2,1)S(1)}, u32[]{:S(2)}, u32[]{:S(2)}) %collective-permute-start.13) | collective-permute-done | bytes 147488 | tf_op jit(solution)/shard_map/ppermute | solution.py:827
  265.0 1.0 fusion.8
  266.0 1.2 collective-permute-start.14
  267.1 1.3 fusion.5
  268.8 1.1 fusion.7
  269.8 1.7 collective-permute-start.11
  271.6 7.5 %collective-permute-done.16 = bf16[4,64,768]{2,1,0:T(8,128)(2,1)S(1)} collective-permute-done((bf16[4,64,768]{2,1,0:T(8,128)(2,1)S(1)}, bf16[4,64,768]{2,1,0:T(8,128)(2,1)S(1)}, u32[]{:S(2)}, u32[]{:S(2)}) %collective-permute-start.16) | collective-permute-done | bytes 393248 | tf_op jit(solution)/shard_map/ppermute | solution.py:827
  279.7 0.9 bitcast_convert_fusion
  280.5 4.4 %collective-permute-done.17 = bf16[2,64,768]{2,1,0:T(8,128)(2,1)S(1)} collective-permute-done((bf16[2,64,768]{2,1,0:T(8,128)(2,1)S(1)}, bf16[2,64,768]{2,1,0:T(8,128)(2,1)S(1)}, u32[]{:S(2)}, u32[]{:S(2)}) %collective-permute-start.17) | collective-permute-done | bytes 196640 | tf_op jit(solution)/shard_map/ppermute | solution.py:827
  285.0 1.8 collective-permute-start.18
  286.9 0.9 copy.44
  287.8 3.9 collective-permute-done.18
  292.4 84.2 %shard_map.337 = (f32[2,48,768]{2,1,0:T(8,128)}, f32[3,48,768]{2,1,0:T(8,128)}, f32[2,48,768]{2,1,0:T(8,128)}, f32[1,48,768]{2,1,0:T(8,128)}, f32[1024,768]{1,0:T(8,128)}, /*index=5*/f32[8,768]{1,0:T(8,128)}) custom-call(bf16[1024,768]{1,0:T(8,128)(2,1)} %refs_0_.1, f32[1,768]{1,0:T(1,128)} %broadcast_in_dim.108.refs_1_, f32[1024,768]{1,0:T(8,128)} %copy-done.4, ...), custom_call_target="tpu_custom_call" | custom-call | flops 13287555072 | bytes 62914560 | tf_op jit(solution)/shard_map/pallas_call | solution.py:682
  376.6 1.5 slice_reduce_fusion
  378.8 1.7 slice_bitcast_fusion.5
  380.5 1.8 slice_bitcast_fusion
  383.8 3.8 copy.52
  (148 shorter events, 20.9 us)
Async XLA Ops:
  0.7 73.2 %copy-start = (bf16[768,768]{1,0:T(8,128)(2,1)S(1)}, bf16[768,768]{1,0:T(8,128)(2,1)}, u32[]{:S(2)}) copy-start(bf16[768,768]{1,0:T(8,128)(2,1)} %param.33) | copy-start | bytes 3538948
  0.7 9.0 %copy-start.3 = (bf16[1024,768]{1,0:T(8,128)(2,1)S(1)}, bf16[1024,768]{1,0:T(8,128)(2,1)}, u32[]{:S(2)}) copy-start(bf16[1024,768]{1,0:T(8,128)(2,1)} %refs_0_.1) | copy-start | bytes 4718596
  0.7 9.0 %copy-start.22 = (f32[768]{0:T(1024)S(1)}, f32[768]{0:T(1024)}, u32[]{:S(2)}) copy-start(f32[768]{0:T(1024)} %param.26) | copy-start | bytes 9220
  0.7 21.0 %collective-permute-start = (bf16[64,768]{1,0:T(8,128)(2,1)}, bf16[64,768]{1,0:T(8,128)(2,1)S(1)}, u32[]{:S(2)}, u32[]{:S(2)}) collective-permute-start(bf16[64,768]{1,0:T(8,128)(2,1)} %param.22), channel_id=1, source_target_pairs={{0,8},{1,9},{2,10},{3,11},{4,12},{5,13},{6,14},{7,15},{8,0},{9,1},... | collective-permute-start | bytes 294920 | tf_op jit(solution)/shard_map/ppermute | solution.py:827
  7.2 12.2 %copy-start.28 = (s32[4,1]{0,1:T(1,128)}, s32[4,1]{0,1:T(1,128)S(1)}, u32[]{:S(2)}) copy-start(s32[4,1]{0,1:T(1,128)S(1)} %reduce-window.6) | copy-start | bytes 52
  9.7 1.3 copy-start.35
  11.0 2.6 copy-start.9
  11.0 2.6 copy-start.36
  13.6 2.7 copy-start.38
  13.6 2.7 copy-start.37
  13.6 3.2 copy-start.30
  16.2 3.2 copy-start.32
  16.2 5.5 %copy-start.10 = (bf16[64,768]{1,0:T(8,128)(2,1)S(1)}, bf16[64,768]{1,0:T(8,128)(2,1)}, u32[]{:S(2)}) copy-start(bf16[64,768]{1,0:T(8,128)(2,1)} %param.22) | copy-start | bytes 294916
  16.9 13.5 %copy-start.31 = (s32[1,4]{1,0:T(1,128)S(1)}, s32[1,4]{1,0:T(1,128)}, u32[]{:S(2)}) copy-start(s32[1,4]{1,0:T(1,128)} %param.23) | copy-start | bytes 52
  16.9 14.1 %copy-start.24 = (bf16[32,12]{0,1:T(8,128)(2,1)S(1)}, bf16[32,12]{0,1:T(8,128)(2,1)}, u32[]{:S(2)}) copy-start(bf16[32,12]{0,1:T(8,128)(2,1)} %param.31) | copy-start | bytes 2308
  17.0 14.7 %copy-start.25 = (f32[768]{0:T(1024)S(1)}, f32[768]{0:T(1024)}, u32[]{:S(2)}) copy-start(f32[768]{0:T(1024)} %param.37) | copy-start | bytes 9220
  20.0 10.5 %copy-start.29 = (s32[4,1]{0,1:T(1,128)S(1)}, s32[4,1]{0,1:T(1,128)}, u32[]{:S(2)}) copy-start(s32[4,1]{0,1:T(1,128)} %copy-done.28) | copy-start | bytes 52
  20.0 8.1 %copy-start.27 = (s32[1,7]{1,0:T(1,128)}, s32[1,7]{1,0:T(1,128)S(1)}, u32[]{:S(2)}) copy-start(s32[1,7]{1,0:T(1,128)S(1)} %get-tuple-element.128) | copy-start | bytes 88
  21.7 6.4 %collective-permute-start.1 = (bf16[128,768]{1,0:T(8,128)(2,1)S(1)}, bf16[128,768]{1,0:T(8,128)(2,1)S(1)}, u32[]{:S(2)}, u32[]{:S(2)}) collective-permute-start(bf16[128,768]{1,0:T(8,128)(2,1)S(1)} %pad_maximum_fusion.3), channel_id=1, source_target_pairs={{0,4},{1,5},{2,6},{3,7},{4,0},{5,1},{6,2},{7,3},{8,12},{9,13},{10,... | collective-permute-start | bytes 589832 | tf_op jit(solution)/shard_map/ppermute | solution.py:827
  28.9 9.9 %collective-permute-start.2 = (bf16[256,768]{1,0:T(8,128)(2,1)}, bf16[256,768]{1,0:T(8,128)(2,1)S(1)}, u32[]{:S(2)}, u32[]{:S(2)}) collective-permute-start(bf16[256,768]{1,0:T(8,128)(2,1)} %pad_maximum_fusion.1), channel_id=1, source_target_pairs={{0,2},{1,3},{2,0},{3,1},{4,6},{5,7},{6,4},{7,5},{8,10},{9,11},{10,... | collective-permute-start | bytes 1179656 | tf_op jit(solution)/shard_map/ppermute | solution.py:827
  34.2 5.5 %copy-start.13 = (bf16[768,1536]{1,0:T(8,128)(2,1)S(1)}, bf16[768,1536]{1,0:T(8,128)(2,1)}, u32[]{:S(2)}) copy-start(bf16[768,1536]{1,0:T(8,128)(2,1)} %constant_dynamic-update-slice_fusion.6) | copy-start | bytes 7077892
  38.6 1.6 copy-start.12
  39.7 28.8 %collective-permute-start.3 = (bf16[512,768]{1,0:T(8,128)(2,1)}, bf16[512,768]{1,0:T(8,128)(2,1)}, u32[]{:S(2)}, u32[]{:S(2)}) collective-permute-start(bf16[512,768]{1,0:T(8,128)(2,1)} %pad_maximum_fusion), channel_id=1, source_target_pairs={{0,1},{1,0},{2,3},{3,2},{4,5},{5,4},{6,7},{7,6},{8,9},{9,8},{10,11... | collective-permute-start | bytes 2359304 | tf_op jit(solution)/shard_map/ppermute | solution.py:827
  40.3 1.4 copy-start.14
  66.4 4.2 %copy-start.33 = (bf16[768,768]{1,0:T(8,128)(2,1)S(1)}, bf16[768,768]{1,0:T(8,128)(2,1)}, u32[]{:S(2)}) copy-start(bf16[768,768]{1,0:T(8,128)(2,1)} %param.30) | copy-start | bytes 3538948
  66.4 4.2 %copy-start.39 = (bf16[1024,768]{1,0:T(8,128)(2,1)S(1)}, bf16[1024,768]{1,0:T(8,128)(2,1)}, u32[]{:S(2)}) copy-start(bf16[1024,768]{1,0:T(8,128)(2,1)} %get-tuple-element.68.o_ref.refs_14_) | copy-start | bytes 4718596
  70.6 1.6 copy-start.21
  72.1 1.7 copy-start.1
  73.8 2.5 copy-start.11
  73.8 2.5 copy-start.15
  73.8 3.3 copy-start.23
  148.5 4.8 %collective-permute-start.4 = (bf16[8,4,48,768]{3,2,1,0:T(8,128)(2,1)}, bf16[8,4,48,768]{3,2,1,0:T(8,128)(2,1)S(1)}, u32[]{:S(2)}, u32[]{:S(2)}) collective-permute-start(bf16[8,4,48,768]{3,2,1,0:T(8,128)(2,1)} %get-tuple-element.74), channel_id=1, source_target_pairs={{0,1},{1,0},{2,3},{3,2},{4,5},{5,4},{6,7},{7,6},{8,9},{9,8},{10,11... | collective-permute-start | bytes 7077896 | tf_op jit(solution)/shard_map/ppermute | solution.py:827
  148.6 8.1 %collective-permute-start.5 = (bf16[16,2,48,768]{3,2,1,0:T(8,128)(2,1)}, bf16[16,2,48,768]{3,2,1,0:T(8,128)(2,1)S(1)}, u32[]{:S(2)}, u32[]{:S(2)}) collective-permute-start(bf16[16,2,48,768]{3,2,1,0:T(8,128)(2,1)} %get-tuple-element.76), channel_id=1, source_target_pairs={{0,1},{1,0},{2,3},{3,2},{4,5},{5,4},{6,7},{7,6},{8,9},{9,8},{10,11... | collective-permute-start | bytes 7077896 | tf_op jit(solution)/shard_map/ppermute | solution.py:827
  156.7 6.6 %copy-start.6 = (bf16[16,2,48,768]{3,2,1,0:T(8,128)(2,1)S(1)}, bf16[16,2,48,768]{3,2,1,0:T(8,128)(2,1)}, u32[]{:S(2)}) copy-start(bf16[16,2,48,768]{3,2,1,0:T(8,128)(2,1)} %get-tuple-element.80) | copy-start | bytes 7077892
  160.1 34.0 %collective-permute-start.6 = (bf16[4,4,48,768]{3,2,1,0:T(8,128)(2,1)}, bf16[4,4,48,768]{3,2,1,0:T(8,128)(2,1)}, u32[]{:S(2)}, u32[]{:S(2)}) collective-permute-start(bf16[4,4,48,768]{3,2,1,0:T(8,128)(2,1)} %get-tuple-element.133), channel_id=1, source_target_pairs={{0,2},{1,3},{2,0},{3,1},{4,6},{5,7},{6,4},{7,5},{8,10},{9,11},{10,... | collective-permute-start | bytes 3538952 | tf_op jit(solution)/shard_map/ppermute | solution.py:827
  165.0 29.1 %collective-permute-start.7 = (bf16[8,2,48,768]{3,2,1,0:T(8,128)(2,1)}, bf16[8,2,48,768]{3,2,1,0:T(8,128)(2,1)}, u32[]{:S(2)}, u32[]{:S(2)}) collective-permute-start(bf16[8,2,48,768]{3,2,1,0:T(8,128)(2,1)} %get-tuple-element.131), channel_id=1, source_target_pairs={{0,16},{16,0},{1,17},{17,1},{2,18},{18,2},{3,19},{19,3},{4,20},{20... | collective-permute-start | bytes 3538952 | tf_op jit(solution)/shard_map/ppermute | solution.py:827
  198.3 9.1 %copy-start.5 = (f32[1024,768]{1,0:T(8,128)S(1)}, f32[1024,768]{1,0:T(8,128)}, u32[]{:S(2)}) copy-start(f32[1024,768]{1,0:T(8,128)} %get-tuple-element.72) | copy-start | bytes 9437188
  199.9 20.9 %copy-start.7 = (bf16[2,4,48,768]{3,2,1,0:T(8,128)(2,1)}, bf16[2,4,48,768]{3,2,1,0:T(8,128)(2,1)S(1)}, u32[]{:S(2)}) copy-start(bf16[2,4,48,768]{3,2,1,0:T(8,128)(2,1)S(1)} %get-tuple-element.92) | copy-start | bytes 1769476
  199.9 7.4 %copy-start.2 = (f32[1024,768]{1,0:T(8,128)S(1)}, f32[1024,768]{1,0:T(8,128)}, u32[]{:S(2)}) copy-start(f32[1024,768]{1,0:T(8,128)} %copy-done.1) | copy-start | bytes 9437188
  200.0 17.8 %collective-permute-start.8 = (bf16[2,4,48,768]{3,2,1,0:T(8,128)(2,1)S(1)}, bf16[2,4,48,768]{3,2,1,0:T(8,128)(2,1)S(1)}, u32[]{:S(2)}, u32[]{:S(2)}) collective-permute-start(bf16[2,4,48,768]{3,2,1,0:T(8,128)(2,1)S(1)} %get-tuple-element.137), channel_id=1, source_target_pairs={{0,4},{1,5},{2,6},{3,7},{4,0},{5,1},{6,2},{7,3},{8,12},{9,13},{10,... | collective-permute-start | bytes 1769480 | tf_op jit(solution)/shard_map/ppermute | solution.py:827
  206.2 14.6 %collective-permute-start.9 = (bf16[4,2,48,768]{3,2,1,0:T(8,128)(2,1)S(1)}, bf16[4,2,48,768]{3,2,1,0:T(8,128)(2,1)S(1)}, u32[]{:S(2)}, u32[]{:S(2)}) collective-permute-start(bf16[4,2,48,768]{3,2,1,0:T(8,128)(2,1)S(1)} %get-tuple-element.135), channel_id=1, source_target_pairs={{0,2},{1,3},{2,0},{3,1},{4,6},{5,7},{6,4},{7,5},{8,10},{9,11},{10,... | collective-permute-start | bytes 1769480 | tf_op jit(solution)/shard_map/ppermute | solution.py:827
  207.3 1.3 copy-start.34
  208.6 2.6 copy-start.4
  208.6 3.4 copy-start.16
  208.6 4.3 %copy-start.40 = (bf16[1024,1536]{1,0:T(8,128)(2,1)S(1)}, bf16[1024,1536]{1,0:T(8,128)(2,1)}, u32[]{:S(2)}) copy-start(bf16[1024,1536]{1,0:T(8,128)(2,1)} %get-tuple-element.91.refs_13_) | copy-start | bytes 9437188
  217.8 5.9 %copy-start.17 = (bf16[2,4,48,768]{3,2,1,0:T(8,128)(2,1)}, bf16[2,4,48,768]{3,2,1,0:T(8,128)(2,1)S(1)}, u32[]{:S(2)}) copy-start(bf16[2,4,48,768]{3,2,1,0:T(8,128)(2,1)S(1)} %collective-permute-done.8) | copy-start | bytes 1769476
  220.9 47.8 %collective-permute-start.10 = (bf16[1,4,48,768]{3,2,1,0:T(8,128)(2,1)S(1)}, bf16[1,4,48,768]{3,2,1,0:T(8,128)(2,1)}, u32[]{:S(2)}, u32[]{:S(2)}) collective-permute-start(bf16[1,4,48,768]{3,2,1,0:T(8,128)(2,1)S(1)} %add_convert_fusion.11), channel_id=1, source_target_pairs={{0,8},{1,9},{2,10},{3,11},{4,12},{5,13},{6,14},{7,15},{8,0},{9,1},... | collective-permute-start | bytes 884744 | tf_op jit(solution)/shard_map/ppermute | solution.py:827
  221.9 31.8 %collective-permute-start.12 = (bf16[2,2,48,768]{3,2,1,0:T(8,128)(2,1)}, bf16[2,2,48,768]{3,2,1,0:T(8,128)(2,1)}, u32[]{:S(2)}, u32[]{:S(2)}) collective-permute-start(bf16[2,2,48,768]{3,2,1,0:T(8,128)(2,1)} %get-tuple-element.142), channel_id=1, source_target_pairs={{0,4},{1,5},{2,6},{3,7},{4,0},{5,1},{6,2},{7,3},{8,12},{9,13},{10,... | collective-permute-start | bytes 884744 | tf_op jit(solution)/shard_map/ppermute | solution.py:827
  223.7 43.4 %collective-permute-start.15 = (bf16[8,64,768]{2,1,0:T(8,128)(2,1)}, bf16[8,64,768]{2,1,0:T(8,128)(2,1)}, u32[]{:S(2)}, u32[]{:S(2)}) collective-permute-start(bf16[8,64,768]{2,1,0:T(8,128)(2,1)} %bitcast.22), channel_id=1, source_target_pairs={{0,1},{1,0},{2,3},{3,2},{4,5},{5,4},{6,7},{7,6},{8,9},{9,8},{10,11... | collective-permute-start | bytes 2359304 | tf_op jit(solution)/shard_map/ppermute | solution.py:827
  224.5 28.5 %copy-start.26 = (f32[1,768]{1,0:T(1,128)S(1)}, f32[1,768]{1,0:T(1,128)}, u32[]{:S(2)}) copy-start(f32[1,768]{1,0:T(1,128)} %get-tuple-element.106) | copy-start | bytes 9220
  254.6 10.4 %collective-permute-start.13 = (bf16[1,2,48,768]{3,2,1,0:T(8,128)(2,1)S(1)}, bf16[1,2,48,768]{3,2,1,0:T(8,128)(2,1)S(1)}, u32[]{:S(2)}, u32[]{:S(2)}) collective-permute-start(bf16[1,2,48,768]{3,2,1,0:T(8,128)(2,1)S(1)} %add_convert_fusion.16), channel_id=1, source_target_pairs={{0,8},{1,9},{2,10},{3,11},{4,12},{5,13},{6,14},{7,15},{8,0},{9,1},... | collective-permute-start | bytes 442376 | tf_op jit(solution)/shard_map/ppermute | solution.py:827
  257.3 11.5 %copy-start.8 = (bf16[2,4,48,768]{3,2,1,0:T(8,128)(2,1)S(1)}, bf16[2,4,48,768]{3,2,1,0:T(8,128)(2,1)}, u32[]{:S(2)}) copy-start(bf16[2,4,48,768]{3,2,1,0:T(8,128)(2,1)} %copy-done.7) | copy-start | bytes 1769476
  257.3 11.4 %copy-start.18 = (bf16[2,4,48,768]{3,2,1,0:T(8,128)(2,1)S(1)}, bf16[2,4,48,768]{3,2,1,0:T(8,128)(2,1)}, u32[]{:S(2)}) copy-start(bf16[2,4,48,768]{3,2,1,0:T(8,128)(2,1)} %copy-done.17) | copy-start | bytes 1769476
  266.0 5.6 %collective-permute-start.14 = (bf16[2,48,768]{2,1,0:T(8,128)(2,1)S(1)}, bf16[2,48,768]{2,1,0:T(8,128)(2,1)S(1)}, u32[]{:S(2)}, u32[]{:S(2)}) collective-permute-start(bf16[2,48,768]{2,1,0:T(8,128)(2,1)S(1)} %fusion.8), channel_id=1, source_target_pairs={{0,16},{16,0},{1,17},{17,1},{2,18},{18,2},{3,19},{19,3},{4,20},{20... | collective-permute-start | bytes 442376 | tf_op jit(solution)/shard_map/ppermute | solution.py:827
  268.4 10.7 %collective-permute-start.16 = (bf16[4,64,768]{2,1,0:T(8,128)(2,1)S(1)}, bf16[4,64,768]{2,1,0:T(8,128)(2,1)S(1)}, u32[]{:S(2)}, u32[]{:S(2)}) collective-permute-start(bf16[4,64,768]{2,1,0:T(8,128)(2,1)S(1)} %get-tuple-element.146), channel_id=1, source_target_pairs={{0,2},{1,3},{2,0},{3,1},{4,6},{5,7},{6,4},{7,5},{8,10},{9,11},{10,... | collective-permute-start | bytes 1179656 | tf_op jit(solution)/shard_map/ppermute | solution.py:827
  269.8 17.0 %collective-permute-start.11 = (bf16[4,48,768]{2,1,0:T(8,128)(2,1)S(1)}, bf16[4,48,768]{2,1,0:T(8,128)(2,1)S(1)}, u32[]{:S(2)}, u32[]{:S(2)}) collective-permute-start(bf16[4,48,768]{2,1,0:T(8,128)(2,1)S(1)} %fusion.7), channel_id=1, source_target_pairs={{0,16},{16,0},{1,17},{17,1},{2,18},{18,2},{3,19},{19,3},{4,20},{20... | collective-permute-start | bytes 884744 | tf_op jit(solution)/shard_map/ppermute | solution.py:827
  279.2 5.7 %collective-permute-start.17 = (bf16[2,64,768]{2,1,0:T(8,128)(2,1)S(1)}, bf16[2,64,768]{2,1,0:T(8,128)(2,1)S(1)}, u32[]{:S(2)}, u32[]{:S(2)}) collective-permute-start(bf16[2,64,768]{2,1,0:T(8,128)(2,1)S(1)} %get-tuple-element.144), channel_id=1, source_target_pairs={{0,4},{1,5},{2,6},{3,7},{4,0},{5,1},{6,2},{7,3},{8,12},{9,13},{10,... | collective-permute-start | bytes 589832 | tf_op jit(solution)/shard_map/ppermute | solution.py:827
  285.0 6.6 %collective-permute-start.18 = (bf16[1,64,768]{2,1,0:T(8,128)(2,1)S(1)}, bf16[1,64,768]{2,1,0:T(8,128)(2,1)S(1)}, u32[]{:S(2)}, u32[]{:S(2)}) collective-permute-start(bf16[1,64,768]{2,1,0:T(8,128)(2,1)S(1)} %add_convert_fusion.18), channel_id=1, source_target_pairs={{0,8},{1,9},{2,10},{3,11},{4,12},{5,13},{6,14},{7,15},{8,0},{9,1},... | collective-permute-start | bytes 294920 | tf_op jit(solution)/shard_map/ppermute | solution.py:827
  376.6 6.4 %copy-start.19 = (f32[2,48,768]{2,1,0:T(8,128)S(1)}, f32[2,48,768]{2,1,0:T(8,128)}, u32[]{:S(2)}) copy-start(f32[2,48,768]{2,1,0:T(8,128)} %get-tuple-element.114) | copy-start | bytes 884740
  383.8 3.8 copy-start.20
where the time goes:
time: 394 us; the launch traced here: 389 us
  Pallas kernels  231 us (59%)
  waiting for transfers between devices  40.8 us (10%)
  local copies, waits for them, and re-layouts  34.8 us (9%)
  starting transfers between devices  27.3 us (7%)
  matrix products  27.1 us (7%)
  other arithmetic  25.9 us (7%)
    pallas_call x1, Pallas kernels, tail_block(): pl.pallas_call(partial(tail_kernel, n_blk, n_dp, plans), in_specs=[vmem_s...  84.2 us
    pallas_call x1, Pallas kernels, feed_block(): pl.pallas_call(partial(feed_kernel, plan_in, plan_out), grid=(FF_STEPS,),...  50.5 us
    ppermute x19, waiting for transfers between devices, swap(): return lax.ppermute(value, axis, [(i, i ^ 1 << bit) for i in range(size)])  40.8 us
    pallas_call x1, Pallas kernels, self_backward(): pl.pallas_call(self_backward_kernel, grid=(PAIRS,), in_specs=[pair_spec()...  27.7 us
    ppermute x19, starting transfers between devices, swap(): return lax.ppermute(value, axis, [(i, i ^ 1 << bit) for i in range(size)])  27.3 us
    pallas_call x1, Pallas kernels, cross_backward(): pl.pallas_call(partial(cross_backward_kernel, passage=passage), in_specs=...  27.2 us
    pallas_call x1, Pallas kernels, self_forward(): pl.pallas_call(self_forward_kernel, grid=(PAIRS,), in_specs=[pair_spec()]...  24.7 us
    dot_general x6, matrix products, dot_nn(): return jnp.dot(a, b, preferred_element_type=jnp.float32)  17.8 us
  transfers between devices with their start and end apart: 19, of which 10 were waited for; matrix products, arithmetic and copies ran while one was open for 12% of the time, Pallas kernels for 20%

commit v1 on v0

--- a/solution.py
+++ b/solution.py
@@ -469,8 +469,8 @@
     dp = [("dp", bit) for bit in range(bits_of(n_dp))]
     if kind == "x":
         return blk[:1] + dp + blk[1:]
-    if kind == "z":
-        return blk[:1] + blk[2:] + blk[1:2]
+    if kind == "y":
+        return blk[:2] + dp + blk[2:]
     return blk
 
 
@@ -490,37 +490,41 @@
 
 
 class Exchange:
-    def __init__(self, count, n_blk, n_dp, kind):
-        if kind == "x" and count % n_dp:
-            kind = "y"
-        self.n_blk, self.n_dp, self.count, self.kind = n_blk, n_dp, count, kind
+    def __init__(self, count, rows, cols, n_blk, n_dp, kind, first=0):
+        if kind in "xy" and count % n_dp:
+            kind = "plain"
+        self.n_blk, self.n_dp, self.count, self.kind, self.first = n_blk, n_dp, count, kind, first
+        self.rows, self.cols = rows, cols
         self.order = place_bits(n_blk, n_dp, kind)
-        self.pieces = n_dp if kind == "x" else 1
+        self.pieces = n_dp if kind in "xy" else 1
         self.slots = n_blk * self.pieces
         self.mats = count // self.pieces
-        self.last = [("dp", bit) for bit in range(bits_of(n_dp))]
+        self.last = [("dp", bit) for bit in range(bits_of(n_dp))] if kind != "near" else []
         self.steps = len(self.order) + len(self.last)
-        self.rows = D // n_blk
-        self.offsets = []
-        at = 0
-        for k in range(len(self.order)):
+        self.held = self.slots >> first
+        self.offsets = {}
+        at = self.held if first else 0
+        for k in range(first, len(self.order)):
             size = self.slots >> (k + 1)
-            self.offsets.append((at, size))
+            self.offsets[k] = (at, size)
             at += size
         for j in range(len(self.last)):
-            size = (1 << j) if kind == "x" else 1
-            self.offsets.append((at, size))
+            size = (1 << j) if self.pieces > 1 else 1
+            self.offsets[len(self.order) + j] = (at, size)
             at += size
         self.received = at
 
     def scratch(self):
-        shape = (self.mats, self.rows, D)
+        shape = (self.mats, self.rows, self.cols)
         return [
-            pltpu.VMEM((self.slots,) + shape, jnp.bfloat16),
+            pltpu.VMEM((max(self.held, self.pieces),) + shape, jnp.bfloat16),
             pltpu.VMEM((self.received,) + shape, jnp.bfloat16),
             pltpu.SemaphoreType.DMA((self.steps,)),
             pltpu.SemaphoreType.DMA((self.steps,)),
         ]
+
+    def out_shape(self):
+        return jax.ShapeDtypeStruct((self.count, self.rows, self.cols), jnp.float32)
 
     def bind(self, refs, out_ref):
         self.buf, self.recv, self.send_sem, self.recv_sem = refs
@@ -552,18 +556,21 @@
     def start(self, k):
         self.copy(k).start()
 
+    def add(self, at, size, final):
+        for s in range(size):
+            for m in range(self.mats):
+                total = self.buf[s, m].astype(jnp.float32) + self.recv[at + s, m].astype(jnp.float32)
+                if final:
+                    self.out[m] = total
+                else:
+                    self.buf[s, m] = total.astype(jnp.bfloat16)
+
     def finish(self, k):
         self.copy(k).wait()
         at, size = self.offsets[k]
         final = k == self.steps - 1
-        if k < len(self.order) or self.kind != "x":
-            for s in range(size):
-                for m in range(self.mats):
-                    total = self.buf[s, m].astype(jnp.float32) + self.recv[at + s, m].astype(jnp.float32)
-                    if final:
-                        self.out[m] = total
-                    else:
-                        self.buf[s, m] = total.astype(jnp.bfloat16)
+        if k < len(self.order) or self.pieces == 1:
+            self.add(at, size, final)
             return
         for s in range(size):
             for m in range(self.mats):
@@ -575,63 +582,221 @@
                     self.out[spot * self.mats + m] = self.buf[s, m].astype(jnp.float32)
 
     def advance(self, k):
+        if k < self.first or k >= self.steps:
+            return
         self.finish(k)
         if k + 1 < self.steps:
             self.start(k + 1)
 
 
+def all_links(n_blk, n_dp):
+    return [("blk", bit) for bit in range(bits_of(n_blk))] + [("dp", bit) for bit in range(bits_of(n_dp))]
+
+
 def enter_barrier(n_blk, n_dp):
     barrier = pltpu.get_barrier_semaphore()
-    links = [("blk", bit) for bit in range(bits_of(n_blk))] + [("dp", bit) for bit in range(bits_of(n_dp))]
+    links = all_links(n_blk, n_dp)
     for axis, bit in links:
         pl.semaphore_signal(barrier, inc=1, device_id=partner(axis, bit), device_id_type=pl.DeviceIdType.MESH)
     pl.semaphore_wait(barrier, len(links))
 
 
-def tail_kernel(n_blk, n_dp, plans, *refs):
-    (x_ref, gain_ref, dy1_ref, act_ref, dq_ref, dk_ref, dv_ref, wq_ref, wk_ref, wv_ref,
-     actc_ref, dqc_ref, enc_ref, dkv_ref, o_ref, oc_ref, e2_ref, small_ref) = refs[:18]
-    outs = refs[18 : 18 + len(plans)]
-    dx_ref, sums_ref = refs[18 + len(plans) : 20 + len(plans)]
-    scratch = refs[20 + len(plans) :]
-    for i, plan in enumerate(plans):
+BLOCKS = 3
+BLOCK = D // BLOCKS
+
+
+def last_plans(n_blk, n_dp):
+    rows = D // n_blk
+    halves = 2
+    feed_in, feed_out = feed_plans(n_blk, n_dp, 2)
+    plans = [
+        feed_in,
+        feed_out,
+        Exchange(3 * halves, rows, D // halves, n_blk, n_dp, "x"),
+        Exchange(2 * halves, rows, D // halves, n_blk, n_dp, "y"),
+    ]
+    for block in range(BLOCKS):
+        plans.append(Exchange(3 * halves, rows, BLOCK // halves, n_blk, n_dp, "xyx"[block]))
+    return plans
+
+
+def feed_plans(n_blk, n_dp, first=0):
+    rows = D // n_blk
+    return (
+        Exchange(4, rows, D, n_blk, n_dp, "y", first),
+        Exchange(4, rows, D, n_blk, n_dp, "x", first),
+    )
+
+
+POOL = 11
+(S_ACTC, S_DQC, S_OC, S_E2, S_Q, S_K, S_V, S_DO, S_O, S_AUG, S_X) = range(POOL)
+S_DQ, S_DK, S_DV, S_ACT = S_ACTC, S_DQC, S_OC, S_E2
+
+
+def last_kernel(n_blk, n_dp, plans, enc_plan, *refs):
+    (x_hbm, dy1_hbm, act_hbm, wq_hbm, wk_hbm, wv_hbm, actc_hbm, dqc_hbm, enc_hbm, dkv_hbm, oc_hbm, e2_hbm,
+     q_hbm, k_hbm, v_hbm, do_hbm, o_hbm, aug_hbm, inkeep_hbm, inrecv_hbm, outkeep_hbm, outrecv_hbm, part_hbm,
+     gain_ref, ak_ref, av_ref, table_ref, small_ref) = refs[:28]
+    every = list(plans) + [enc_plan]
+    outs = refs[28 : 28 + len(every)]
+    dx_hbm, sums_ref = refs[28 + len(every) : 30 + len(every)]
+    scratch = refs[30 + len(every) :]
+    for i, plan in enumerate(every):
         plan.bind(scratch[4 * i : 4 * i + 4], outs[i])
-    tot_ref, got_ref, tsend, trecv = scratch[4 * len(plans) :]
+    (pool, dy1_ref, act_t, bias_ref, g_ref, gfar_ref, dqt_ref,
+     tot_ref, got_ref, tsend, trecv, load_sem, store_sem) = scratch[4 * len(every) :]
+    feed_in, feed_out, crossx, crossy, self0, self1, self2 = plans
+    selfs = (self0, self1, self2)
+
+    loads = {}
+
+    def load(name, src, dst):
+        loads[name] = pltpu.make_async_copy(src, dst, load_sem.at[len(loads)])
+        loads[name].start()
+
+    def slot(index):
+        return pool.at[index]
+
+    load("actc", actc_hbm, slot(S_ACTC))
+    load("dqc", dqc_hbm, slot(S_DQC))
+    for plan, keep, got, name in (
+        (feed_out, outkeep_hbm, outrecv_hbm, "out"),
+        (feed_in, inkeep_hbm, inrecv_hbm, "in"),
+    ):
+        load(name + "keep", keep, plan.buf.at[pl.ds(0, plan.held)])
+        load(name + "recv", got, plan.recv.at[pl.ds(0, plan.held)])
+    spans = enc_hbm.shape[0] // LEN
+    spare = (S_Q, S_K, S_V, S_DO, S_AUG, S_X)
+    for n in range(spans):
+        rows = pl.ds(n * LEN, LEN)
+        load(("enc", n), enc_hbm.at[rows], slot(spare[3 * n]))
+        load(("dk", n), dkv_hbm.at[rows, pl.ds(0, D)], slot(spare[3 * n + 1]))
+        load(("dv", n), dkv_hbm.at[rows, pl.ds(D, D)], slot(spare[3 * n + 2]))
+    load("part", part_hbm, enc_plan.buf)
+    load("oc", oc_hbm, slot(S_OC))
+    load("e2", e2_hbm, slot(S_E2))
+    load("o", o_hbm, slot(S_O))
+    load("dy1", dy1_hbm, dy1_ref)
     enter_barrier(n_blk, n_dp)
-    crossx, crossy, selfx, selfy = plans
-
-    crossx.put(0, dot_tn(actc_ref[...], dqc_ref[...]))
-    crossx.put(1, dot_tn(enc_ref[...], dkv_ref[:, :D]))
+
+    def begin_feed(plan, name):
+        loads[name + "keep"].wait()
+        loads[name + "recv"].wait()
+        plan.add(0, plan.held, False)
+        plan.start(plan.first)
+
+    def put_halves(plan, index, value):
+        half = plan.cols
+        for c in range(2):
+            plan.put(2 * index + c, value[:, c * half : (c + 1) * half])
+
+    begin_feed(feed_out, "out")
+    begin_feed(feed_in, "in")
+    loads["actc"].wait()
+    loads["dqc"].wait()
+    put_halves(crossx, 0, dot_tn(pool[S_ACTC], pool[S_DQC]))
+    for w, name in ((1, "dk"), (2, "dv")):
+        total = None
+        for n in range(spans):
+            if w == 1:
+                loads["enc", n].wait()
+            loads[name, n].wait()
+            part = dot_tn(pool[spare[3 * n]], pool[spare[3 * n + w]])
+            total = part if total is None else total + part
+        put_halves(crossx, w, total)
     crossx.start(0)
-    crossy.put(0, dot_tn(enc_ref[...], dkv_ref[:, D:]))
-    crossy.put(1, dot_tn(oc_ref[...], e2_ref[...]))
-    crossy.put(2, dot_tn(o_ref[...], dy1_ref[...].astype(jnp.bfloat16)))
+    for name, src, index in (
+        ("q", q_hbm, S_Q), ("k", k_hbm, S_K), ("v", v_hbm, S_V), ("do", do_hbm, S_DO), ("aug", aug_hbm, S_AUG), ("x", x_hbm, S_X),
+    ):
+        load(name, src, slot(index))
+    loads["part"].wait()
+    enc_plan.start(0)
+    loads["oc"].wait()
+    loads["e2"].wait()
+    put_halves(crossy, 0, dot_tn(pool[S_OC], pool[S_E2]))
+    loads["o"].wait()
+    loads["dy1"].wait()
+    put_halves(crossy, 1, dot_tn(pool[S_O], dy1_ref[...].astype(jnp.bfloat16)))
     crossy.start(0)
+    load("act", act_hbm, slot(S_ACT))
     crossx.advance(0)
-    selfx.put(0, dot_tn(act_ref[...], dq_ref[...]))
-    selfx.put(1, dot_tn(act_ref[...], dk_ref[...]))
-    selfx.start(0)
+    for name in ("q", "k", "v", "do", "aug"):
+        loads[name].wait()
+    loads["act"].wait()
+    act_t[...] = pool[S_ACT].T
     crossy.advance(0)
-    selfy.put(0, dot_tn(act_ref[...], dv_ref[...]))
-    selfy.start(0)
-    selfx.advance(0)
+    enc_plan.advance(0)
+
+    offsets = lax.broadcasted_iota(jnp.int32, (1, WIN), 1) - TILE
+    chosen = bucket_vector(None, jnp.maximum(offsets, 0))
+
+    def pair_body(p):
+        lanes = pl.ds(pl.multiple_of(p * LANES, LANES), LANES)
+        dq, dk, dv, sums = self_pair_backward(
+            pool[S_Q, :, lanes], pool[S_K, :, lanes], pool[S_V, :, lanes], pool[S_DO, :, lanes], pool[S_O, :, lanes],
+            pool[S_AUG, :, lanes], ak_ref[...], av_ref[...], table_ref[p], offsets, chosen,
+            bias_ref, g_ref, gfar_ref, dqt_ref,
+            lambda rows, value: pool.__setitem__((S_DK, rows, lanes), value),
+            lambda rows, value: pool.__setitem__((S_DV, rows, lanes), value),
+        )
+        pool[S_DQ, :, lanes] = dq
+        for head in range(2):
+            tot_ref[3 + 2 * p + head] = jnp.concatenate(
+                [sums[head], jnp.zeros((1, D - BUCKETS), jnp.float32)], axis=1
+            )
+
+    tot_ref[0:3] = small_ref[...]
+    rounds = {
+        0: [],
+        1: [(feed_out, 2), (feed_in, 2)],
+        2: [(crossy, 1)],
+        3: [(crossx, 1), (feed_out, 3), (feed_in, 3), (enc_plan, 1)],
+        4: [(crossy, 2), (self0, 0)],
+        5: [(feed_out, 4), (feed_in, 4), (enc_plan, 2)],
+    }
+    per_block = PAIRS // BLOCKS
+    for block in range(BLOCKS):
+        for inner in range(per_block):
+            p = block * per_block + inner
+            for plan, k in rounds[p]:
+                plan.advance(k)
+            pair_body(p)
+        cols = slice(block * BLOCK, (block + 1) * BLOCK)
+        for w, index in enumerate((S_DQ, S_DK, S_DV)):
+            put_halves(selfs[block], w, dot_nn(act_t[...], pool[index, :, cols]))
+        selfs[block].start(0)
+    wq, wk, wv = slot(S_Q), slot(S_K), slot(S_V)
+    for name, src, index in (("wq", wq_hbm, S_Q), ("wk", wk_hbm, S_K), ("wv", wv_hbm, S_V)):
+        load(name, src, pool.at[index, pl.ds(0, D)])
+    crossx.advance(2)
+    self1.advance(0)
+    for name in ("wq", "wk", "wv", "x"):
+        loads[name].wait()
+    pending = [
+        [(crossy, 3), (self0, 1), (enc_plan, 3), (self2, 0)],
+        [(crossx, 3), (feed_out, 5), (feed_in, 5)],
+        [(self1, 1), (crossy, 4), (self0, 2)],
+        [(crossx, 4), (self2, 1)],
+    ]
     gain_sum = jnp.zeros((1, D), jnp.float32)
+    stores = []
     for i, r in enumerate(range(0, LEN, ROWS)):
         rows = slice(r, r + ROWS)
-        da = dot_nt(dq_ref[rows], wq_ref[...]) + dot_nt(dk_ref[rows], wk_ref[...]) + dot_nt(dv_ref[rows], wv_ref[...])
-        x = x_ref[rows].astype(jnp.float32)
+        da = (
+            dot_nt(pool[S_DQ, rows], pool[S_Q, :D])
+            + dot_nt(pool[S_DK, rows], pool[S_K, :D])
+            + dot_nt(pool[S_DV, rows], pool[S_V, :D])
+        )
+        x = pool[S_X, rows].astype(jnp.float32)
         inverse = norm_parts(x)
         gain_sum = gain_sum + jnp.sum(da * x * inverse, axis=0, keepdims=True)
-        dx_ref[rows] = dy1_ref[rows] + norm_back(x, inverse, gain_ref[...], da)
-        if i == 0:
-            selfy.advance(0)
-        if i == 1:
-            crossx.advance(1)
-        if i == 2:
-            crossy.advance(1)
-    tot_ref[...] = small_ref[...]
-    tot_ref[0:1] = gain_sum
-    links = [("blk", bit) for bit in range(bits_of(n_blk))] + [("dp", bit) for bit in range(bits_of(n_dp))]
+        dy1_ref[rows] = dy1_ref[rows] + norm_back(x, inverse, gain_ref[...], da)
+        stores.append(pltpu.make_async_copy(dy1_ref.at[rows], dx_hbm.at[rows], store_sem.at[i]))
+        stores[-1].start()
+        for plan, k in pending[i]:
+            plan.advance(k)
+    tot_ref[0] = gain_sum
+    links = all_links(n_blk, n_dp)
 
     def small_copy(j):
         axis, bit = links[j]
@@ -645,52 +810,140 @@
         )
 
     small_copy(0).start()
-    longest = max(plan.steps for plan in plans)
-    for k in range(1, longest):
-        for plan in (selfx, selfy, crossx, crossy):
-            step = k if plan in (selfx, selfy) else k + 1
-            if step < plan.steps:
-                plan.advance(step)
-        if k - 1 < len(links):
-            small_copy(k - 1).wait()
-            tot_ref[...] = tot_ref[...] + got_ref[k - 1]
-            if k < len(links):
-                small_copy(k).start()
-    for j in range(longest - 1, len(links)):
-        small_copy(j).wait()
-        tot_ref[...] = tot_ref[...] + got_ref[j]
-        if j + 1 < len(links):
-            small_copy(j + 1).start()
+    done = {feed_in: 5, feed_out: 5, crossx: 4, crossy: 4, enc_plan: 3, self0: 2, self1: 1, self2: 1}
+    longest = max(plan.steps for plan in every)
+    j = 0
+    while True:
+        for plan in (self2, self1, self0, crossx, crossy, feed_out, feed_in, enc_plan):
+            done[plan] += 1
+            plan.advance(done[plan])
+        if j < len(links):
+            small_copy(j).wait()
+            tot_ref[...] = tot_ref[...] + got_ref[j]
+            j += 1
+            if j < len(links):
+                small_copy(j).start()
+        if j == len(links) and all(done[plan] >= plan.steps - 1 for plan in every):
+            break
     sums_ref[...] = tot_ref[...]
-
-
-def tail_block(n_blk, n_dp, *args):
-    plans = [
-        Exchange(2, n_blk, n_dp, "x"),
-        Exchange(3, n_blk, n_dp, "y"),
-        Exchange(2, n_blk, n_dp, "x"),
-        Exchange(1, n_blk, n_dp, "y"),
-    ]
-    links = bits_of(n_blk) + bits_of(n_dp)
-    scratch = [item for plan in plans for item in plan.scratch()]
+    for store in stores:
+        store.wait()
+
+
+def self_pair_backward(q_raw, k_raw, v_raw, do_raw, o_raw, aug, ak, av, table, offsets, chosen,
+                       bias_ref, g_ref, gfar_ref, dqt_ref, put_dk, put_dv):
+    line = dot_nn(table, chosen)
+    line = jnp.where(offsets >= 0, line, NEG)
+    far = table[:, BUCKETS - 1 :].astype(jnp.float32)
+    for head in range(2):
+        spread = jnp.broadcast_to(line[head : head + 1], (TILE, WIN))
+        bias_ref[head] = pltpu.roll(spread, 0, 1, stride=1, stride_axis=0)[:, TILE:]
+    g_ref[...] = jnp.zeros_like(g_ref)
+    gfar_ref[...] = jnp.zeros_like(gfar_ref)
+    dqt_ref[...] = jnp.zeros_like(dqt_ref)
+    product = do_raw.astype(jnp.float32) * o_raw.astype(jnp.float32)
+    deltas = []
+    for head in range(2):
+        half = in_half(LEN, head)
+        deltas.append(jnp.sum(jnp.where(half, product, 0.0), axis=1, keepdims=True))
+    aug_do = (-triple_lanes(deltas[0], deltas[1], LEN)).astype(jnp.bfloat16)
+    q_scaled = q_raw * jnp.bfloat16(SCALE)
+    k_t = k_raw.T
+    accs = {}
+    for head in range(2):
+        half = in_half(LEN, head)
+        q = jnp.where(half, q_scaled, aug)
+        k = jnp.where(half, k_raw, ak)
+        v = jnp.where(half, v_raw, av)
+        do = jnp.where(half, do_raw, aug_do)
+        for j in range(LEN // TILE):
+            lo = j * TILE
+            hi = min(LEN, (j + 3) * TILE)
+            width = hi - lo
+            near = min(2 * TILE, width)
+            scores = dot_nt(k[lo : lo + TILE], q[lo:hi])
+            parts = [scores[:, :near] + bias_ref[head][:, :near]]
+            if width > near:
+                parts.append(scores[:, near:] + far[head : head + 1])
+            scores = parts[0] if len(parts) == 1 else jnp.concatenate(parts, axis=1)
+            probs = jnp.exp(scores)
+            grad_probs = dot_nt(v[lo : lo + TILE], do[lo:hi])
+            grad_scores = probs * grad_probs
+            g_ref[head, :, :near] += grad_scores[:, :near]
+            if width > near:
+                gfar_ref[head] += jnp.sum(grad_scores[:, near:].reshape(TILE // 8, 8, TILE), axis=0)
+            ds = grad_scores.astype(jnp.bfloat16)
+            accs[j, head] = (dot_nn(ds, q[lo:hi]), dot_nn(probs.astype(jnp.bfloat16), do[lo:hi]))
+            dqt_ref[head * HD : (head + 1) * HD, lo:hi] += dot_nn(
+                k_t[head * HD : (head + 1) * HD, lo : lo + TILE], ds
+            )
+            if head == 1:
+                lower = in_half(TILE, 0)
+                rows = slice(lo, lo + TILE)
+                put_dk(rows, jnp.where(lower, accs[j, 0][0], accs[j, 1][0]).astype(jnp.bfloat16))
+                put_dv(rows, jnp.where(lower, accs[j, 0][1], accs[j, 1][1]).astype(jnp.bfloat16))
+    dq = (dqt_ref[...] * SCALE).T.astype(jnp.bfloat16)
+    rows = []
+    for head in range(2):
+        total = jnp.zeros((8, WIN), jnp.float32)
+        pad = jnp.zeros((8, TILE), jnp.float32)
+        for a in range(TILE // 8):
+            strip = jnp.concatenate([pad, g_ref[head, 8 * a : 8 * a + 8, :]], axis=1)
+            if a:
+                strip = pltpu.roll(strip, WIN - 8 * a, 1)
+            total = total + strip
+        line_sum = jnp.zeros((1, WIN), jnp.float32)
+        for s in range(8):
+            one = total[s : s + 1]
+            line_sum = line_sum + (pltpu.roll(one, WIN - s, 1) if s else one)
+        rows.append(line_sum)
+    lines = jnp.concatenate(rows, axis=0)
+    lines = jnp.where(offsets >= 0, lines, 0.0)
+    high, mid, low = split3(lines)
+    sums = sum(dot_nt(part.astype(jnp.bfloat16), chosen) for part in (high, mid, low))
+    lane32 = lax.broadcasted_iota(jnp.int32, (1, BUCKETS), 1)
+    tables = []
+    for head in range(2):
+        far_sum = jnp.sum(gfar_ref[head])
+        tables.append(sums[head : head + 1] + jnp.where(lane32 == BUCKETS - 1, far_sum, 0.0))
+    return dq, None, None, tables
+
+
+def any_spec():
+    return pl.BlockSpec(memory_space=pl.ANY)
+
+
+def last_block(n_blk, n_dp, plans, enc_plan, big, little, keys):
+    every = list(plans) + [enc_plan]
+    links = len(all_links(n_blk, n_dp))
+    scratch = [item for plan in every for item in plan.scratch()]
     scratch += [
-        pltpu.VMEM((8, D), jnp.float32),
-        pltpu.VMEM((links, 8, D), jnp.float32),
+        pltpu.VMEM((POOL, LEN, D), jnp.bfloat16),
+        pltpu.VMEM((LEN, D), jnp.float32),
+        pltpu.VMEM((D, LEN), jnp.bfloat16),
+        pltpu.VMEM((2, TILE, 2 * TILE), jnp.float32),
+        pltpu.VMEM((2, TILE, 2 * TILE), jnp.float32),
+        pltpu.VMEM((2, 8, TILE), jnp.float32),
+        pltpu.VMEM((LANES, LEN), jnp.float32),
+        pltpu.VMEM((3 + H, 1, D), jnp.float32),
+        pltpu.VMEM((links, 3 + H, 1, D), jnp.float32),
         pltpu.SemaphoreType.DMA((links,)),
         pltpu.SemaphoreType.DMA((links,)),
+        pltpu.SemaphoreType.DMA((len(big) + 3 * (keys // LEN) - 2 + 1,)),
+        pltpu.SemaphoreType.DMA((LEN // ROWS,)),
     ]
     return pl.pallas_call(
-        partial(tail_kernel, n_blk, n_dp, plans),
-        in_specs=[vmem_spec()] * len(args),
-        out_specs=[vmem_spec()] * (len(plans) + 2),
-        out_shape=[jax.ShapeDtypeStruct((plan.count, plan.rows, D), jnp.float32) for plan in plans]
-        + [jax.ShapeDtypeStruct((LEN, D), jnp.float32), jax.ShapeDtypeStruct((8, D), jnp.float32)],
+        partial(last_kernel, n_blk, n_dp, plans, enc_plan),
+        in_specs=[any_spec()] * len(big) + [vmem_spec()] * len(little),
+        out_specs=[vmem_spec()] * len(every) + [any_spec(), vmem_spec()],
+        out_shape=[plan.out_shape() for plan in every]
+        + [jax.ShapeDtypeStruct((LEN, D), jnp.float32), jax.ShapeDtypeStruct((3 + H, 1, D), jnp.float32)],
         scratch_shapes=scratch,
         compiler_params=pltpu.CompilerParams(
             vmem_limit_bytes=VMEM_LIMIT, collective_id=1, has_side_effects=True
         ),
-        cost_estimate=pl.CostEstimate(flops=22 * LEN * D * D, bytes_accessed=80 * LEN * D, transcendentals=0),
-    )(*args)
+        cost_estimate=pl.CostEstimate(flops=40 * LEN * D * D, bytes_accessed=80 * LEN * D, transcendentals=0),
+    )(*big, *little)
 
 
 FF_STEPS = 4
@@ -757,9 +1010,10 @@
     for t in range(0, plan_in.n_blk, 2):
         even = dw1[t * plan_in.rows : (t + 1) * plan_in.rows]
         odd = dw1[(t + 1) * plan_in.rows : (t + 2) * plan_in.rows]
-        slot = rest_slot(t, 0, plan_in.order)
-        isend_ref[slot, 0] = jnp.where(even_core, odd, even).astype(jnp.bfloat16)
-        ikeep_ref[slot, 0] = jnp.where(even_core, even, odd).astype(jnp.bfloat16)
+        slot = rest_slot(t, step // plan_in.mats, plan_in.order)
+        inner = step % plan_in.mats
+        isend_ref[slot, inner] = jnp.where(even_core, odd, even).astype(jnp.bfloat16)
+        ikeep_ref[slot, inner] = jnp.where(even_core, even, odd).astype(jnp.bfloat16)
 
     @pl.when(step == FF_STEPS - 1)
     def _():
@@ -782,10 +1036,9 @@
 def feed_block(y1, oc, wco, gain, g, w1, w2, plan_in, plan_out):
     ff = w1.shape[1]
     cols = ff // FF_STEPS
-    fixed = lambda shape: pl.BlockSpec(shape, lambda c: (0,) * len(shape))
+    fixed = lambda shape: pl.BlockSpec(memory_space=pltpu.VMEM)
     half_in = (plan_in.slots // 2, plan_in.mats, plan_in.rows, D)
     half_out = (plan_out.slots // 2, plan_out.mats, plan_out.rows, D)
-    in_spec = pl.BlockSpec((half_in[0], 1) + half_in[2:], lambda c: (0, c, 0, 0))
     like = jax.ShapeDtypeStruct
     return pl.pallas_call(
         partial(feed_kernel, plan_in, plan_out),
@@ -796,7 +1049,7 @@
             pl.BlockSpec((cols, D), lambda c: (c, 0)),
         ],
         out_specs=[
-            fixed((LEN, D)), in_spec, in_spec, fixed(half_out), fixed(half_out),
+            fixed((LEN, D)), fixed(half_in), fixed(half_in), fixed(half_out), fixed(half_out),
             fixed((LEN, D)), fixed((LEN, D)), fixed((LEN, D)), fixed((1, D)),
         ],
         out_shape=[
@@ -841,16 +1094,6 @@
         out = jnp.concatenate([out, swap(out, "blk", bit, n_blk)], axis=0)
         masks = masks + [mask | (1 << bit) for mask in masks]
     return out, masks
-
-
-def scatter_slots(value, n_blk):
-    terms = [value]
-    for bit in range(bits_of(n_blk)):
-        half = terms[0].shape[0] // 2
-        send = total_of([t[half:] for t in terms]).astype(jnp.bfloat16)
-        kept = total_of([t[:half] for t in terms]).astype(jnp.bfloat16)
-        terms = [kept, swap(send, "blk", bit, n_blk)]
-    return total_of(terms)[0]
 
 
 def scatter_step(terms, axis, bit, n):
@@ -915,8 +1158,7 @@
     pair_all = dot_nn(encoder_all, pair_weight).astype(jnp.bfloat16)
     attn_cross, aug_cross = cross_forward(order, items, query_cross, pair_all, passage)
 
-    plan_in = Exchange(4, n_blk, n_dp, "y")
-    plan_out = Exchange(4, n_blk, n_dp, "x")
+    plan_in, plan_out = feed_plans(n_blk, n_dp)
     (block_out, in_send, in_keep, out_send, out_keep, grad_resid_cross, round_cross, grad_attn_cross, gain_feed) = feed_block(
         resid_self, attn_cross, cross_output, feed_gain2, cotangent, feed_input_weight, feed_out, plan_in, plan_out
     )
@@ -930,78 +1172,45 @@
         order, items, query_cross, pair_all, grad_attn_cross, attn_cross, aug_cross, passage
     )
     (terms_in, terms_out), dqc, dkv = lax.optimization_barrier(((next_in, next_out), dqc, dkv))
-    next_in, next_out = step(plan_in, terms_in, 2), step(plan_out, terms_out, 2)
     encoder_part = dot_nt(dkv, pair_weight).astype(jnp.bfloat16)
     da_cross = dot_nt(dqc, cross_query)
     gain_cross = jnp.sum(da_cross * resid_self * inv_cross, axis=0)
     grad_resid_self = grad_resid_cross + norm_back(resid_self, inv_cross, cross_gain2, da_cross)
     round_self = grad_resid_self.astype(jnp.bfloat16)
     grad_attn_self = dot_nt(round_self, self_output).astype(jnp.bfloat16)
-    (terms_in, terms_out), grad_attn_self, encoder_part = lax.optimization_barrier(
-        ((next_in, next_out), grad_attn_self, encoder_part)
+    small = jnp.stack([jnp.zeros((1, D), jnp.float32), gain_cross[None], gain_feed])
+    enc_plan = Exchange(1, passage, D, n_blk, n_dp, "near")
+    big = (
+        decoder_rows, grad_resid_self, act_self, self_query, self_key, self_value, act_cross, dqc, encoder_all, dkv,
+        attn_cross, round_cross, query_self, key_self, value_self, grad_attn_self, attn_self, aug_self,
+        terms_in[0], terms_in[1], terms_out[0], terms_out[1], encoder_part.reshape(n_blk, 1, passage, D),
     )
-    for k in range(3, len(plan_in.order)):
-        terms_in = step(plan_in, terms_in, k)
-    for k in range(3, len(plan_out.order)):
-        terms_out = step(plan_out, terms_out, k)
-    total_in = total_of(terms_in)[0]
-    for bit in range(bits_of(n_dp)):
-        own = total_in.astype(jnp.bfloat16)
-        total_in = total_of([own, swap(own, "dp", bit, n_dp)])
-    sum_feed_in = jnp.swapaxes(total_in, 0, 1).reshape(D // n_blk, -1)
-    total_out = total_of(terms_out)[0]
-    if plan_out.kind == "x":
-        for bit in range(bits_of(n_dp)):
-            own = total_out.astype(jnp.bfloat16)
-            other = swap(own, "dp", bit, n_dp)
-            low = (lax.axis_index("dp") >> bit) & 1 == 0
-            total_out = jnp.concatenate([jnp.where(low, own, other), jnp.where(low, other, own)], axis=0)
-        total_out = total_out.astype(jnp.float32)
-    else:
-        for bit in range(bits_of(n_dp)):
-            own = total_out.astype(jnp.bfloat16)
-            total_out = total_of([own, swap(own, "dp", bit, n_dp)])
-    sum_feed_out = total_out.reshape(-1, D)
-    grad_encoder = scatter_slots(encoder_part.reshape(n_blk, passage, D), n_blk)
-    dq, dk, dv, table_parts = self_backward(
-        query_self, key_self, value_self, grad_attn_self, attn_self, aug_self, ak, av, table_pairs
+    feed_in, feed_out_sum, crossx, crossy, self0, self1, self2, grad_encoder, grad_decoder, sums = last_block(
+        n_blk, n_dp, last_plans(n_blk, n_dp), enc_plan, big, (self_gain2, ak, av, table_pairs, small), encoder_all.shape[0]
     )
-    sum_feed_in, sum_feed_out, grad_encoder, dq, dk, dv = lax.optimization_barrier(
-        (sum_feed_in, sum_feed_out, grad_encoder, dq, dk, dv)
-    )
-    small = jnp.concatenate(
-        [
-            jnp.zeros((1, D), jnp.float32),
-            gain_cross[None],
-            gain_feed,
-            jnp.pad(table_parts.reshape(1, H * BUCKETS), ((0, 0), (0, D - H * BUCKETS))),
-            jnp.zeros((4, D), jnp.float32),
-        ],
-        axis=0,
-    )
-    crossx, crossy, selfx, selfy, grad_decoder, sums = tail_block(
-        n_blk, n_dp,
-        decoder_rows, self_gain2, grad_resid_self, act_self, dq, dk, dv, self_query, self_key, self_value,
-        act_cross, dqc, encoder_all, dkv, attn_self, attn_cross, round_cross, small,
-    )
+    rows = D // n_blk
+    wide = lambda units: jnp.concatenate(units, axis=1)
+    self_w = [wide([part[2 * w + c] for part in (self0, self1, self2) for c in range(2)]) for w in range(3)]
+    cross_w = [wide([crossx[2 * w], crossx[2 * w + 1]]) for w in range(3)]
+    out_w = [wide([crossy[2 * w], crossy[2 * w + 1]]) for w in range(2)]
     return (
         block_out,
         grad_decoder,
-        grad_encoder,
-        sums[0],
-        selfx[0],
-        selfx[1],
-        selfy[0],
-        crossy[2],
-        sums[3, : H * BUCKETS].reshape(H, BUCKETS).T,
-        sums[1],
-        crossx[0],
-        crossx[1],
-        crossy[0],
-        crossy[1],
-        sums[2],
-        sum_feed_in,
-        sum_feed_out,
+        grad_encoder[0],
+        sums[0, 0],
+        self_w[0],
+        self_w[1],
+        self_w[2],
+        out_w[1],
+        sums[3:, 0, :BUCKETS].T,
+        sums[1, 0],
+        cross_w[0],
+        cross_w[1],
+        cross_w[2],
+        out_w[0],
+        sums[2, 0],
+        wide([feed_in[m] for m in range(4)]),
+        feed_out_sum.reshape(-1, D),
     )
 
 

time: 394 us -> 328 us (0.83)
  waiting for transfers between devices: 40.8 us -> 12 us
  starting transfers between devices: 27.3 us -> 10.4 us
  Pallas kernels: 231 us -> 222 us
  local copies, waits for them, and re-layouts: 34.8 us -> 28.7 us
  other arithmetic: 25.9 us -> 21 us
    ppermute x19 -> x8, waiting for transfers between devices: 40.8 us -> 12 us  [swap(): return lax.ppermute(value, axis, [(i, i ^ 1 << bit) for i in range(size)])]
    ppermute x19 -> x8, starting transfers between devices: 27.3 us -> 10.4 us  [swap(): return lax.ppermute(value, axis, [(i, i ^ 1 << bit) for i in range(size)])]
    pallas_call x2 -> x1, Pallas kernels: 112 us -> 96.1 us  [last_block(): pl.pallas_call(partial(last_kernel, n_blk, n_dp, plans, enc_plan), in_spe...]
    convert_element_type x7 -> x0, other arithmetic: 5.19 us -> none  [the longest x2 1.39 us: scatter_slots(): kept = total_of([t[:half] for t in terms]).astype(jnp.bfloat16)]
    concatenate x1 -> x6, other arithmetic: 0.03 us -> 4.28 us  [per_device(): wide = lambda units: jnp.concatenate(units, axis=1)]
    convert_element_type x6 -> x2, other arithmetic: 9.35 us -> 5.48 us  [scatter_step(): send = total_of([t[half:] for t in terms]).astype(jnp.bfloat16)]
    unnamed x89 -> x104, local copies, waits for them, and re-layouts: 17.7 us -> 17.8 us
  transfers between devices with their start and end apart: 19 -> 8, of which waited for: 10 -> 4; matrix products, arithmetic and copies ran while one was open for 12% -> 9% of each run, Pallas kernels for 20% -> 17%
where the time goes in v1:
time: 328 us; the launch traced here: 324 us
  Pallas kernels  222 us (68%)
  local copies, waits for them, and re-layouts  28.7 us (9%)
  matrix products  28.5 us (9%)
  other arithmetic  21 us (6%)
  waiting for transfers between devices  12 us (4%)
  starting transfers between devices  10.4 us (3%)
    pallas_call x1, Pallas kernels, last_block(): pl.pallas_call(partial(last_kernel, n_blk, n_dp, plans, enc_plan), in_spe...  96.1 us
    pallas_call x1, Pallas kernels, feed_block(): pl.pallas_call(partial(feed_kernel, plan_in, plan_out), grid=(FF_STEPS,),...  51.5 us
    pallas_call x1, Pallas kernels, cross_backward(): pl.pallas_call(partial(cross_backward_kernel, passage=passage), in_specs=...  30.9 us
    pallas_call x1, Pallas kernels, self_forward(): pl.pallas_call(self_forward_kernel, grid=(PAIRS,), in_specs=[pair_spec()]...  24.7 us
    pallas_call x1, Pallas kernels, cross_forward(): pl.pallas_call(partial(cross_forward_kernel, passage=passage), in_specs=[...  19.3 us
    unnamed x104, local copies, waits for them, and re-layouts  17.8 us
    dot_general x6, matrix products, dot_nn(): return jnp.dot(a, b, preferred_element_type=jnp.float32)  17.7 us
    ppermute x8, waiting for transfers between devices, swap(): return lax.ppermute(value, axis, [(i, i ^ 1 << bit) for i in range(size)])  12 us
  transfers between devices with their start and end apart: 8, of which 4 were waited for; matrix products, arithmetic and copies ran while one was open for 9% of the time, Pallas kernels for 17%

profile of v1, /device:TPU:0, one launch (start us, length us, event | category | flops | bytes accessed | tf_op | source)
XLA Modules:
  0.0 324.5 jit_solution(9596936386676707428)
XLA Ops:
  0.7 4.1 %collective-permute-start = (bf16[64,768]{1,0:T(8,128)(2,1)}, bf16[64,768]{1,0:T(8,128)(2,1)S(1)}, u32[]{:S(2)}, u32[]{:S(2)}) collective-permute-start(bf16[64,768]{1,0:T(8,128)(2,1)} %param.22), channel_id=1, source_target_pairs={{0,8},{1,9},{2,10},{3,11},{4,12},{5,13},{6,14},{7,15},{8,0},{9,1},... | collective-permute-start | bytes 294920 | tf_op jit(solution)/shard_map/ppermute | solution.py:1080
  4.8 1.6 constant_dynamic-update-slice_fusion.4
  6.4 0.8 reduce-window.6
  7.2 0.7 subtract_add_fusion.1
  7.9 1.8 fusion
  10.1 0.8 copy-done.39
  11.0 2.5 convolution_convert_fusion.6.q_ref.refs_12_
  13.5 2.6 convolution_convert_fusion.5.k_ref.refs_13_
  16.9 2.4 constant_dynamic-update-slice_fusion.6
  19.9 1.1 select_convert_fusion
  21.0 0.6 select_reduce_fusion.order_ref
  21.6 1.6 collective-permute-start.1
  23.8 4.3 %collective-permute-done.1 = bf16[128,768]{1,0:T(8,128)(2,1)S(1)} collective-permute-done((bf16[128,768]{1,0:T(8,128)(2,1)S(1)}, bf16[128,768]{1,0:T(8,128)(2,1)S(1)}, u32[]{:S(2)}, u32[]{:S(2)}) %collective-permute-start.1) | collective-permute-done | bytes 196640 | tf_op jit(solution)/shard_map/ppermute | solution.py:1080
  28.0 0.8 pad_maximum_fusion.2
  28.8 1.5 collective-permute-start.2
  30.3 0.6 add_reduce_fusion
  32.2 0.6 stack_broadcast_in_dim.9
  32.8 1.3 stack.16.item_ref
  34.1 4.4 %convolution_convert_fusion.4.v_ref.refs_14_ = bf16[1024,768]{1,0:T(8,128)(2,1)} fusion(bf16[1024,768]{1,0:T(8,128)(2,1)} %copy-done.8, bf16[768,768]{1,0:T(8,128)(2,1)} %refs_5_.1), kind=kOutput, calls=%fused_computation.19 | convolution fusion | flops 1208745984 | bytes 4325376 | tf_op jit(solution)/shard_map/dot_general | solution.py:29
  38.7 0.9 pad_maximum_fusion
  40.2 1.4 copy-done.13
  41.6 24.7 %shard_map.332 = (bf16[1024,768]{1,0:T(8,128)(2,1)}, bf16[1024,768]{1,0:T(8,128)(2,1)}) custom-call(bf16[1024,768]{1,0:T(8,128)(2,1)} %convolution_convert_fusion.6.q_ref.refs_12_, bf16[1024,768]{1,0:T(8,128)(2,1)} %convolution_convert_fusion.5.k_ref.refs_13_, bf16[1024,768]{1,0:T(8,128)(2,1)} %convolution_convert_fusion.4.v_ref.refs_14_, ...), custom_call_target="tpu_custom_call" | custom-call | flops 3221225472 | bytes 7864320 | tf_op jit(solution)/shard_map/pallas_call | solution.py:131
  66.3 0.6 constant_dynamic-update-slice_fusion.3
  66.9 0.7 constant_dynamic-update-slice_fusion.2
  67.6 0.8 constant_dynamic-update-slice_fusion.1
  68.4 2.1 constant_dynamic-update-slice_fusion.refs_8_
  70.5 1.5 multiply_reduce_fusion.2
  72.4 1.3 copy-done.1
  73.7 2.5 convolution_convert_fusion.3.q_ref
  76.3 0.7 copy-done.24
  77.0 4.0 %convolution_convert_fusion.kv_ref = bf16[1024,1536]{1,0:T(8,128)(2,1)} fusion(bf16[1024,768]{1,0:T(8,128)(2,1)S(1)} %copy-done.24, bf16[768,1536]{1,0:T(8,128)(2,1)S(1)} %copy-done.14), kind=kOutput, calls=%fused_computation.3 | convolution fusion | flops 2417491968 | bytes 7077888 | tf_op jit(solution)/shard_map/dot_general | solution.py:29
  81.0 19.3 %shard_map.333 = (bf16[1024,768]{1,0:T(8,128)(2,1)}, bf16[1024,768]{1,0:T(8,128)(2,1)}) custom-call(s32[16]{0:T(128)} %select_reduce_fusion.order_ref, s32[5,7]{1,0:T(8,128)} %stack.16.item_ref, bf16[1024,768]{1,0:T(8,128)(2,1)} %convolution_convert_fusion.3.q_ref, bf16[1024,1536]{1,0:T(8,128)(2,1)} %convolution_convert_fusion.kv_ref), custom_call_target="tpu_custom_call" | custom-call | flops 1610612736 | bytes 7864320 | tf_op jit(solution)/shard_map/pallas_call | solution.py:300
  100.3 51.5 %shard_map.334 = (bf16[1024,768]{1,0:T(8,128)(2,1)}, bf16[16,2,48,768]{3,2,1,0:T(8,128)(2,1)}, bf16[16,2,48,768]{3,2,1,0:T(8,128)(2,1)}, bf16[16,2,48,768]{3,2,1...) custom-call(f32[1024,768]{1,0:T(8,128)} %copy-done.1, ...), custom_call_target="tpu_custom_call" | custom-call | flops 28991029248 | bytes 31457280 | tf_op jit(solution)/shard_map/pallas_call | solution.py:1043
  152.4 4.2 %collective-permute-done.4 = bf16[16,2,48,768]{3,2,1,0:T(8,128)(2,1)S(1)} collective-permute-done((bf16[16,2,48,768]{3,2,1,0:T(8,128)(2,1)}, bf16[16,2,48,768]{3,2,1,0:T(8,128)(2,1)S(1)}, u32[]{:S(2)}, u32[]{:S(2)}) %collective-permute-start.4) | collective-permute-done | bytes 2359328 | tf_op jit(solution)/shard_map/ppermute | solution.py:1080
  156.6 3.4 %collective-permute-done.5 = bf16[16,2,48,768]{3,2,1,0:T(8,128)(2,1)S(1)} collective-permute-done((bf16[16,2,48,768]{3,2,1,0:T(8,128)(2,1)}, bf16[16,2,48,768]{3,2,1,0:T(8,128)(2,1)S(1)}, u32[]{:S(2)}, u32[]{:S(2)}) %collective-permute-start.5) | collective-permute-done | bytes 2359328 | tf_op jit(solution)/shard_map/ppermute | solution.py:1080
  160.0 3.6 %add_convert_fusion.2 = (bf16[8,2,48,768]{3,2,1,0:T(8,128)(2,1)S(1)}, bf16[8,2,48,768]{3,2,1,0:T(8,128)(2,1)}) fusion(bf16[16,2,48,768]{3,2,1,0:T(8,128)(2,1)S(1)} %collective-permute-done.4, bf16[16,2,48,768]{3,2,1,0:T(8,128)(2,1)} %get-tuple-element.66), kind=kLoop, calls=%fused_computation.14 | loop fusion | flops 4718592 | bytes 7077888 | tf_op jit(solution)/shard_map/convert_element_type | solution.py:1101
  163.6 1.9 add_convert_fusion
  165.5 2.5 collective-permute-start.7
  168.6 30.9 %shard_map.335 = (bf16[1024,768]{1,0:T(8,128)(2,1)}, bf16[1024,1536]{1,0:T(8,128)(2,1)}) custom-call(s32[16]{0:T(128)} %select_reduce_fusion.order_ref, s32[5,7]{1,0:T(8,128)} %stack.16.item_ref, bf16[1024,768]{1,0:T(8,128)(2,1)} %convolution_convert_fusion.3.q_ref, bf16[1024,1536]{1,0:T(8,128)(2,1)} %convolution_convert_fusion.kv_ref, ...), custom_call_target="tpu_custom_call" | custom-call | flops 4026531840 | bytes 14155776 | tf_op jit(solution)/shard_map/pallas_call | solution.py:389
  199.5 4.3 %multiply_reduce_fusion = (f32[768]{0:T(1024)S(1)}, f32[1024]{0:T(1024)S(1)}, f32[1024,768]{1,0:T(8,128)S(1)}) fusion(f32[1024,768]{1,0:T(8,128)} %copy-done.1, f32[1024]{0:T(1024)S(1)} %add_rsqrt_fusion, f32[768]{0:T(1024)S(1)} %copy-done.22, bf16[1024,768]{1,0:T(8,128)(2,1)} %get-tuple-element.74.refs_7_, bf16[768,768]{1,0:T(8,128)(2,1)S(1)} %copy-done), kind=kOutput, calls=%fused_computation.7 | convolution fusion | flops 1212676352 | bytes 9058304 | tf_op jit(solution)/shard_map/dot_general | solution.py:33
  203.8 0.6 subtract_add_fusion.refs_1_
  204.5 0.6 copy-done.38
  205.1 2.6 convolution_convert_fusion.2.refs_15_
  207.7 0.8 copy-done.15
  208.5 0.9 copy-done.44
  209.4 4.0 %convolution_convert_fusion.1 = bf16[1024,768]{1,0:T(8,128)(2,1)} fusion(bf16[1024,1536]{1,0:T(8,128)(2,1)S(1)} %copy-done.44, bf16[768,1536]{1,0:T(8,128)(2,1)S(1)} %copy-done.15), kind=kOutput, calls=%fused_computation.16 | convolution fusion | flops 2416705536 | bytes 7077888 | tf_op jit(solution)/shard_map/dot_general | solution.py:33
  213.4 0.7 pad_maximum_fusion.9.refs_27_
  214.1 0.7 broadcast_in_dim.102.refs_25_
  214.8 96.1 %shard_map.336 = (f32[4,48,768]{2,1,0:T(8,128)}, f32[4,48,768]{2,1,0:T(8,128)}, f32[6,48,384]{2,1,0:T(8,128)}, f32[4,48,384]{2,1,0:T(8,128)}, f32[6,48,128]{2,1,...) custom-call(bf16[1024,768]{1,0:T(8,128)(2,1)} %refs_0_.1, ...), custom_call_target="tpu_custom_call" | custom-call | flops 24159191040 | bytes 62914560 | tf_op jit(solution)/shard_map/pallas_call | solution.py:935
  311.0 1.4 slice_reduce_fusion
  312.3 0.7 slice.166
  313.0 0.8 constant_dynamic-update-slice_fusion.24
  313.8 1.0 slice_bitcast_fusion.5
  314.8 0.6 copy.43
  315.4 1.1 slice_bitcast_fusion.7
  316.6 0.7 pad_maximum_fusion.4
  317.3 0.7 pad_maximum_fusion.5
  318.0 0.7 pad_maximum_fusion.6
  318.7 0.7 pad_maximum_fusion.7
  319.3 0.7 pad_maximum_fusion.8
  320.1 0.9 pad_maximum_fusion.1
  321.1 1.7 copy.67
  322.7 0.7 copy.68
  323.4 0.8 copy.69
  (125 shorter events, 6.0 us)
Async XLA Ops:
  0.7 73.1 %copy-start = (bf16[768,768]{1,0:T(8,128)(2,1)S(1)}, bf16[768,768]{1,0:T(8,128)(2,1)}, u32[]{:S(2)}) copy-start(bf16[768,768]{1,0:T(8,128)(2,1)} %param.33) | copy-start | bytes 3538948
  0.7 9.0 %copy-start.3 = (bf16[1024,768]{1,0:T(8,128)(2,1)S(1)}, bf16[1024,768]{1,0:T(8,128)(2,1)}, u32[]{:S(2)}) copy-start(bf16[1024,768]{1,0:T(8,128)(2,1)} %refs_0_.1) | copy-start | bytes 4718596
  0.7 9.0 %copy-start.23 = (f32[768]{0:T(1024)S(1)}, f32[768]{0:T(1024)}, u32[]{:S(2)}) copy-start(f32[768]{0:T(1024)} %param.26) | copy-start | bytes 9220
  0.7 20.9 %collective-permute-start = (bf16[64,768]{1,0:T(8,128)(2,1)}, bf16[64,768]{1,0:T(8,128)(2,1)S(1)}, u32[]{:S(2)}, u32[]{:S(2)}) collective-permute-start(bf16[64,768]{1,0:T(8,128)(2,1)} %param.22), channel_id=1, source_target_pairs={{0,8},{1,9},{2,10},{3,11},{4,12},{5,13},{6,14},{7,15},{8,0},{9,1},... | collective-permute-start | bytes 294920 | tf_op jit(solution)/shard_map/ppermute | solution.py:1080
  7.2 12.1 %copy-start.32 = (s32[4,1]{0,1:T(1,128)}, s32[4,1]{0,1:T(1,128)S(1)}, u32[]{:S(2)}) copy-start(s32[4,1]{0,1:T(1,128)S(1)} %reduce-window.6) | copy-start | bytes 52
  9.7 1.3 copy-start.39
  11.0 2.5 copy-start.8
  11.0 2.5 copy-start.40
  13.5 2.7 copy-start.42
  13.5 2.7 copy-start.41
  13.5 3.2 copy-start.34
  16.1 3.2 copy-start.36
  16.1 5.5 %copy-start.9 = (bf16[64,768]{1,0:T(8,128)(2,1)S(1)}, bf16[64,768]{1,0:T(8,128)(2,1)}, u32[]{:S(2)}) copy-start(bf16[64,768]{1,0:T(8,128)(2,1)} %param.22) | copy-start | bytes 294916
  16.9 13.4 %copy-start.35 = (s32[1,4]{1,0:T(1,128)S(1)}, s32[1,4]{1,0:T(1,128)}, u32[]{:S(2)}) copy-start(s32[1,4]{1,0:T(1,128)} %param.23) | copy-start | bytes 52
  16.9 14.1 %copy-start.28 = (bf16[32,12]{0,1:T(8,128)(2,1)S(1)}, bf16[32,12]{0,1:T(8,128)(2,1)}, u32[]{:S(2)}) copy-start(bf16[32,12]{0,1:T(8,128)(2,1)} %param.31) | copy-start | bytes 2308
  16.9 14.7 %copy-start.29 = (f32[768]{0:T(1024)S(1)}, f32[768]{0:T(1024)}, u32[]{:S(2)}) copy-start(f32[768]{0:T(1024)} %param.37) | copy-start | bytes 9220
  19.9 10.4 %copy-start.33 = (s32[4,1]{0,1:T(1,128)S(1)}, s32[4,1]{0,1:T(1,128)}, u32[]{:S(2)}) copy-start(s32[4,1]{0,1:T(1,128)} %copy-done.32) | copy-start | bytes 52
  19.9 8.1 %copy-start.31 = (s32[1,7]{1,0:T(1,128)}, s32[1,7]{1,0:T(1,128)S(1)}, u32[]{:S(2)}) copy-start(s32[1,7]{1,0:T(1,128)S(1)} %get-tuple-element.104) | copy-start | bytes 88
  21.6 6.4 %collective-permute-start.1 = (bf16[128,768]{1,0:T(8,128)(2,1)S(1)}, bf16[128,768]{1,0:T(8,128)(2,1)S(1)}, u32[]{:S(2)}, u32[]{:S(2)}) collective-permute-start(bf16[128,768]{1,0:T(8,128)(2,1)S(1)} %pad_maximum_fusion.3), channel_id=1, source_target_pairs={{0,4},{1,5},{2,6},{3,7},{4,0},{5,1},{6,2},{7,3},{8,12},{9,13},{10,... | collective-permute-start | bytes 589832 | tf_op jit(solution)/shard_map/ppermute | solution.py:1080
  28.8 9.9 %collective-permute-start.2 = (bf16[256,768]{1,0:T(8,128)(2,1)}, bf16[256,768]{1,0:T(8,128)(2,1)S(1)}, u32[]{:S(2)}, u32[]{:S(2)}) collective-permute-start(bf16[256,768]{1,0:T(8,128)(2,1)} %pad_maximum_fusion.2), channel_id=1, source_target_pairs={{0,2},{1,3},{2,0},{3,1},{4,6},{5,7},{6,4},{7,5},{8,10},{9,11},{10,... | collective-permute-start | bytes 1179656 | tf_op jit(solution)/shard_map/ppermute | solution.py:1080
  34.1 5.5 %copy-start.12 = (bf16[768,1536]{1,0:T(8,128)(2,1)S(1)}, bf16[768,1536]{1,0:T(8,128)(2,1)}, u32[]{:S(2)}) copy-start(bf16[768,1536]{1,0:T(8,128)(2,1)} %constant_dynamic-update-slice_fusion.6) | copy-start | bytes 7077892
  38.5 1.6 copy-start.11
  39.6 28.8 %collective-permute-start.3 = (bf16[512,768]{1,0:T(8,128)(2,1)}, bf16[512,768]{1,0:T(8,128)(2,1)}, u32[]{:S(2)}, u32[]{:S(2)}) collective-permute-start(bf16[512,768]{1,0:T(8,128)(2,1)} %pad_maximum_fusion), channel_id=1, source_target_pairs={{0,1},{1,0},{2,3},{3,2},{4,5},{5,4},{6,7},{7,6},{8,9},{9,8},{10,11... | collective-permute-start | bytes 2359304 | tf_op jit(solution)/shard_map/ppermute | solution.py:1080
  40.2 1.4 copy-start.13
  66.3 4.2 %copy-start.37 = (bf16[768,768]{1,0:T(8,128)(2,1)S(1)}, bf16[768,768]{1,0:T(8,128)(2,1)}, u32[]{:S(2)}) copy-start(bf16[768,768]{1,0:T(8,128)(2,1)} %param.30) | copy-start | bytes 3538948
  66.3 4.2 %copy-start.43 = (bf16[1024,768]{1,0:T(8,128)(2,1)S(1)}, bf16[1024,768]{1,0:T(8,128)(2,1)}, u32[]{:S(2)}) copy-start(bf16[1024,768]{1,0:T(8,128)(2,1)} %get-tuple-element.56.refs_16_) | copy-start | bytes 4718596
  70.5 1.6 copy-start.22
  72.1 1.7 copy-start.1
  73.7 2.6 copy-start.10
  73.7 2.6 copy-start.14
  73.7 3.3 %copy-start.24 = (bf16[1024,768]{1,0:T(8,128)(2,1)S(1)}, bf16[1024,768]{1,0:T(8,128)(2,1)}, u32[]{:S(2)}) copy-start(bf16[1024,768]{1,0:T(8,128)(2,1)} %constant_dynamic-update-slice_fusion.refs_8_) | copy-start | bytes 4718596
  151.8 4.8 %collective-permute-start.4 = (bf16[16,2,48,768]{3,2,1,0:T(8,128)(2,1)}, bf16[16,2,48,768]{3,2,1,0:T(8,128)(2,1)S(1)}, u32[]{:S(2)}, u32[]{:S(2)}) collective-permute-start(bf16[16,2,48,768]{3,2,1,0:T(8,128)(2,1)} %get-tuple-element.62), channel_id=1, source_target_pairs={{0,1},{1,0},{2,3},{3,2},{4,5},{5,4},{6,7},{7,6},{8,9},{9,8},{10,11... | collective-permute-start | bytes 7077896 | tf_op jit(solution)/shard_map/ppermute | solution.py:1080
  151.9 8.1 %collective-permute-start.5 = (bf16[16,2,48,768]{3,2,1,0:T(8,128)(2,1)}, bf16[16,2,48,768]{3,2,1,0:T(8,128)(2,1)S(1)}, u32[]{:S(2)}, u32[]{:S(2)}) collective-permute-start(bf16[16,2,48,768]{3,2,1,0:T(8,128)(2,1)} %get-tuple-element.64), channel_id=1, source_target_pairs={{0,1},{1,0},{2,3},{3,2},{4,5},{5,4},{6,7},{7,6},{8,9},{9,8},{10,11... | collective-permute-start | bytes 7077896 | tf_op jit(solution)/shard_map/ppermute | solution.py:1080
  160.0 3.6 %copy-start.7 = (bf16[16,2,48,768]{3,2,1,0:T(8,128)(2,1)S(1)}, bf16[16,2,48,768]{3,2,1,0:T(8,128)(2,1)}, u32[]{:S(2)}) copy-start(bf16[16,2,48,768]{3,2,1,0:T(8,128)(2,1)} %get-tuple-element.68) | copy-start | bytes 7077892
  163.6 35.9 %collective-permute-start.6 = (bf16[8,2,48,768]{3,2,1,0:T(8,128)(2,1)S(1)}, bf16[8,2,48,768]{3,2,1,0:T(8,128)(2,1)}, u32[]{:S(2)}, u32[]{:S(2)}) collective-permute-start(bf16[8,2,48,768]{3,2,1,0:T(8,128)(2,1)S(1)} %get-tuple-element.109), channel_id=1, source_target_pairs={{0,2},{1,3},{2,0},{3,1},{4,6},{5,7},{6,4},{7,5},{8,10},{9,11},{10,... | collective-permute-start | bytes 3538952 | tf_op jit(solution)/shard_map/ppermute | solution.py:1080
  165.5 34.0 %collective-permute-start.7 = (bf16[8,2,48,768]{3,2,1,0:T(8,128)(2,1)S(1)}, bf16[8,2,48,768]{3,2,1,0:T(8,128)(2,1)}, u32[]{:S(2)}, u32[]{:S(2)}) collective-permute-start(bf16[8,2,48,768]{3,2,1,0:T(8,128)(2,1)S(1)} %get-tuple-element.107), channel_id=1, source_target_pairs={{0,16},{16,0},{1,17},{17,1},{2,18},{18,2},{3,19},{19,3},{4,20},{20... | collective-permute-start | bytes 3538952 | tf_op jit(solution)/shard_map/ppermute | solution.py:1080
  199.5 4.3 %copy-start.2 = (f32[1024,768]{1,0:T(8,128)S(1)}, f32[1024,768]{1,0:T(8,128)}, u32[]{:S(2)}) copy-start(f32[1024,768]{1,0:T(8,128)} %copy-done.1) | copy-start | bytes 9437188
  199.5 4.3 %copy-start.5 = (f32[1024,768]{1,0:T(8,128)S(1)}, f32[1024,768]{1,0:T(8,128)}, u32[]{:S(2)}) copy-start(f32[1024,768]{1,0:T(8,128)} %get-tuple-element.60) | copy-start | bytes 9437188
  203.8 1.3 copy-start.38
  205.1 2.6 copy-start.6
  205.1 3.4 %copy-start.15 = (bf16[768,1536]{1,0:T(8,128)(2,1)S(1)}, bf16[768,1536]{1,0:T(8,128)(2,1)}, u32[]{:S(2)}) copy-start(bf16[768,1536]{1,0:T(8,128)(2,1)} %copy-done.13) | copy-start | bytes 7077892
  205.1 4.3 %copy-start.44 = (bf16[1024,1536]{1,0:T(8,128)(2,1)S(1)}, bf16[1024,1536]{1,0:T(8,128)(2,1)}, u32[]{:S(2)}) copy-start(bf16[1024,1536]{1,0:T(8,128)(2,1)} %get-tuple-element.75.refs_9_) | copy-start | bytes 9437188
  209.4 4.0 %copy-start.30 = (f32[1,768]{1,0:T(1,128)S(1)}, f32[1,768]{1,0:T(1,128)}, u32[]{:S(2)}) copy-start(f32[1,768]{1,0:T(1,128)} %get-tuple-element.82) | copy-start | bytes 9220
  310.9 5.6 %copy-start.17 = (f32[4,48,768]{2,1,0:T(8,128)S(1)}, f32[4,48,768]{2,1,0:T(8,128)}, u32[]{:S(2)}) copy-start(f32[4,48,768]{2,1,0:T(8,128)} %get-tuple-element.91) | copy-start | bytes 1769476
  315.4 4.6 %copy-start.21 = (f32[6,48,128]{2,1,0:T(8,128)S(1)}, f32[6,48,128]{2,1,0:T(8,128)}, u32[]{:S(2)}) copy-start(f32[6,48,128]{2,1,0:T(8,128)} %get-tuple-element.86) | copy-start | bytes 442372
  316.6 3.5 %copy-start.20 = (f32[6,48,128]{2,1,0:T(8,128)S(1)}, f32[6,48,128]{2,1,0:T(8,128)}, u32[]{:S(2)}) copy-start(f32[6,48,128]{2,1,0:T(8,128)} %get-tuple-element.87) | copy-start | bytes 442372
  316.6 3.5 %copy-start.19 = (f32[6,48,128]{2,1,0:T(8,128)S(1)}, f32[6,48,128]{2,1,0:T(8,128)}, u32[]{:S(2)}) copy-start(f32[6,48,128]{2,1,0:T(8,128)} %get-tuple-element.88) | copy-start | bytes 442372
  317.3 3.8 %copy-start.4 = (f32[1024,768]{1,0:T(8,128)S(1)}, f32[1024,768]{1,0:T(8,128)}, u32[]{:S(2)}) copy-start(f32[1024,768]{1,0:T(8,128)} %get-tuple-element.169) | copy-start | bytes 9437188
  320.1 2.6 copy-start.25
  320.1 2.6 copy-start.26
  320.1 2.6 copy-start.27
  321.1 1.7 copy-start.18
  321.1 2.4 copy-start.16
